TPU v7x, 32 devices: a whole 2x2x4 slice. The times are simulated.
32 devices in a mesh: dp: 8 (over z, x), mlp: 4 (over y, core).
Axes of the slice: x: 2, y: 2, z: 4, core: 2. Of those that a mesh axis runs over, the one named last changes fastest.
Arguments:
- tokens: bfloat16 [2, 6304, 768], P(None, ('dp', 'mlp')), may hold values from -6 to 6
- keep_mask: int32 [2, 6304], P(None, ('dp', 'mlp')), may hold values 0 or 1
- position_index: int32 [197, 197], replicated, may hold values from 0 to 731
- cotangent: bfloat16 [2, 6304, 768], P(None, ('dp', 'mlp')), may hold values from -6 to 6
- first_gain: float32 [768], replicated, may hold values from 0.5 to 1.5
- first_shift: float32 [768], replicated, may hold values from -4 to 4
- inner_weight: bfloat16 [768, 2304], P(('dp', 'mlp')), may hold values from -0.21875 to 0.21875
- query_bias: float32 [768], replicated, may hold values from -6 to 6
- value_bias: float32 [768], replicated, may hold values from -6 to 6
- outer_weight: bfloat16 [768, 768], P(('dp', 'mlp')), may hold values from -0.875 to 0.875
- outer_bias: float32 [768], replicated, may hold values from -4 to 4
- attend_scale: float32 [768], replicated, may hold values from 0.5 to 1.5
- second_gain: float32 [768], replicated, may hold values from 0.5 to 1.5
- second_shift: float32 [768], replicated, may hold values from -4 to 4
- up_weight: bfloat16 [768, 3072], P('dp', 'mlp'), may hold values from -0.21875 to 0.21875
- up_bias: float32 [3072], replicated, may hold values from -6 to 6
- down_weight: bfloat16 [3072, 768], P('mlp', 'dp'), may hold values from -0.109375 to 0.109375
- down_bias: float32 [768], replicated, may hold values from -4 to 4
- feed_scale: float32 [768], replicated, may hold values from 0.5 to 1.5
- position_table: float32 [732, 12], replicated, may hold values from -6 to 6
Outputs:
- result: bfloat16 [2, 6304, 768], P(None, ('dp', 'mlp'))
- gradient_tokens: bfloat16 [2, 6304, 768], P(None, ('dp', 'mlp'))
- gradient_inner: float32 [768, 2304], P(('dp', 'mlp'))
- gradient_outer: float32 [768, 768], P(('dp', 'mlp'))
- gradient_up: float32 [768, 3072], P('dp', 'mlp')
- gradient_down: float32 [3072, 768], P('mlp', 'dp')
- gradient_first_gain: float32 [768], replicated
- gradient_first_shift: float32 [768], replicated
- gradient_query_bias: float32 [768], replicated
- gradient_value_bias: float32 [768], replicated
- gradient_outer_bias: float32 [768], replicated
- gradient_attend_scale: float32 [768], replicated
- gradient_second_gain: float32 [768], replicated
- gradient_second_shift: float32 [768], replicated
- gradient_up_bias: float32 [3072], replicated
- gradient_down_bias: float32 [768], replicated
- gradient_feed_scale: float32 [768], replicated
- gradient_table: float32 [732, 12], replicated
All inputs are finite; a program needn't handle non-finite values. No bound on the sum of `keep_mask` on one device may be relied on, other than what follows from the above.
Results may differ from a plain program's by a relative error of at most 0.014.
Values may be sent and summed in bfloat16 or wider, within the bound.
A program may use at most 192 MiB of HBM per device.

v0:
```python
import jax
import jax.numpy as jnp
from jax import lax
from jax.sharding import PartitionSpec as P

EPS = 1e-06
ROOT_HALF = 0.7071067811865476
DENSITY = 0.3989422804014327


def layer_norm(values, gain, shift):
    mean = jnp.mean(values, -1, keepdims=True)
    centred = values - mean
    variance = jnp.mean(centred * centred, -1, keepdims=True)
    scaled = lax.rsqrt(variance + EPS)
    unit = centred * scaled
    return (unit * gain + shift, unit, scaled)


def norm_back(upstream, unit, scaled, gain):
    inner = upstream * gain
    first = jnp.mean(inner, -1, keepdims=True)
    second = jnp.mean(inner * unit, -1, keepdims=True)
    return (
        scaled * (inner - first - unit * second),
        jnp.sum(upstream * unit, 0),
        jnp.sum(upstream, 0),
    )


def gelu_pair(pre):
    cumul = 0.5 * (1.0 + lax.erf(pre * ROOT_HALF))
    return (pre * cumul, cumul + pre * jnp.exp(-0.5 * pre * pre) * DENSITY)


def fetch(inner_weight, outer_weight, up_weight, down_weight):
    inner_full, outer_full = (
        lax.all_gather(inner_weight, ("dp", "mlp"), axis=0, tiled=True),
        lax.all_gather(outer_weight, ("dp", "mlp"), axis=0, tiled=True),
    )
    up_full, down_full = (
        lax.all_gather(up_weight, "dp", axis=0, tiled=True),
        lax.all_gather(down_weight, "dp", axis=1, tiled=True),
    )
    return (inner_full, outer_full, up_full, down_full)


def contract_rows(left, right):
    return lax.dot_general(
        left, right, (((0,), (0,)), ((), ())), preferred_element_type=jnp.float32
    )


def contract_cols(left, right):
    return lax.dot_general(
        left, right, (((1,), (1,)), ((), ())), preferred_element_type=jnp.float32
    )


def logits_of(query, keys, bias, allowed, factor):
    raw = jnp.einsum("qhd,khd->hqk", query, keys, preferred_element_type=jnp.float32) * factor
    return jnp.where(allowed, raw + bias, -1e30)


def body(
    tokens,
    keep_mask,
    position_index,
    cotangent,
    first_gain,
    first_shift,
    inner_weight,
    query_bias,
    value_bias,
    outer_weight,
    outer_bias,
    attend_scale,
    second_gain,
    second_shift,
    up_weight,
    up_bias,
    down_weight,
    down_bias,
    feed_scale,
    position_table,
):
    micro, rows, width = tokens.shape
    heads = position_table.shape[1]
    head_dim = width // heads
    factor = head_dim ** (-0.5)
    entries = position_table.shape[0]
    columns = up_weight.shape[1]
    col_start = lax.axis_index("mlp") * columns
    up_local = lax.dynamic_slice_in_dim(up_bias, col_start, columns, 0)
    shift_vector = jnp.concatenate([query_bias, jnp.zeros_like(query_bias), value_bias])
    table_by_head = jnp.transpose(position_table)
    bias = table_by_head[:, position_index]
    seen = jnp.arange(rows)
    diagonal = seen[:, None] == seen[None, :]
    flat_index = position_index.reshape(rows * rows)
    zero_width = jnp.zeros((width,), jnp.float32)
    sum_inner = jnp.zeros((width, 3 * width), jnp.float32)
    sum_outer = jnp.zeros((width, width), jnp.float32)
    sum_up = jnp.zeros((width, columns), jnp.float32)
    sum_down = jnp.zeros((columns, width), jnp.float32)
    sum_table_heads = jnp.zeros((heads, entries), jnp.float32)
    sum_up_bias = jnp.zeros((columns,), jnp.float32)
    sum_first_gain = zero_width
    sum_first_shift = zero_width
    sum_query_bias = zero_width
    sum_value_bias = zero_width
    sum_outer_bias = zero_width
    sum_attend_scale = zero_width
    sum_second_gain = zero_width
    sum_second_shift = zero_width
    sum_down_bias = zero_width
    sum_feed_scale = zero_width
    results = []
    input_grads = []
    for index in range(micro):
        inner_full, outer_full, up_full, down_full = fetch(
            inner_weight, outer_weight, up_weight, down_weight
        )
        source = tokens[index].astype(jnp.float32)
        allowed = jnp.logical_or(keep_mask[index][None, :] == 1, diagonal)[None]
        normed_one, unit_one, scaled_one = layer_norm(source, first_gain, first_shift)
        normed_one = normed_one.astype(jnp.bfloat16)
        projected = (
            jnp.dot(normed_one, inner_full, preferred_element_type=jnp.float32) + shift_vector
        ).astype(jnp.bfloat16)
        query = projected[:, :width].reshape(rows, heads, head_dim)
        keys = projected[:, width : 2 * width].reshape(rows, heads, head_dim)
        values = projected[:, 2 * width :].reshape(rows, heads, head_dim)
        logits = logits_of(query, keys, bias, allowed, factor)
        top = jnp.max(logits, -1, keepdims=True)
        expd = jnp.exp(logits - top)
        total = jnp.sum(expd, -1, keepdims=True)
        probs = expd / total
        log_total = top + jnp.log(total)
        mixed = jnp.einsum(
            "hqk,khd->qhd", probs.astype(jnp.bfloat16), values, preferred_element_type=jnp.float32
        )
        mixed = mixed.reshape(rows, width).astype(jnp.bfloat16)
        attend = jnp.dot(mixed, outer_full, preferred_element_type=jnp.float32) + outer_bias
        resid = source + attend_scale * attend
        normed_two, unit_two, scaled_two = layer_norm(resid, second_gain, second_shift)
        normed_two = normed_two.astype(jnp.bfloat16)
        sequence_rows = lax.all_gather(normed_two, "mlp", axis=0, tiled=True)
        pre = jnp.dot(sequence_rows, up_full, preferred_element_type=jnp.float32) + up_local
        active, slope = gelu_pair(pre)
        hidden = active.astype(jnp.bfloat16)
        feed = (
            lax.psum_scatter(
                jnp.dot(hidden, down_full, preferred_element_type=jnp.float32).astype(jnp.bfloat16),
                "mlp",
                scatter_dimension=0,
                tiled=True,
            ).astype(jnp.float32)
            + down_bias
        )
        results.append((resid + feed_scale * feed).astype(jnp.bfloat16))
        inner_full, outer_full, up_full, down_full = fetch(
            inner_weight, outer_weight, up_weight, down_weight
        )
        upstream = cotangent[index].astype(jnp.float32)
        sum_feed_scale = sum_feed_scale + jnp.sum(feed * upstream, 0)
        dfeed = feed_scale * upstream
        sum_down_bias = sum_down_bias + jnp.sum(dfeed, 0)
        upstream_all = lax.all_gather(dfeed.astype(jnp.bfloat16), "mlp", axis=0, tiled=True)
        sum_down = sum_down + contract_rows(hidden, upstream_all)
        dpre = (contract_cols(upstream_all, down_full) * slope).astype(jnp.bfloat16)
        sum_up_bias = sum_up_bias + jnp.sum(dpre.astype(jnp.float32), 0)
        sum_up = sum_up + contract_rows(sequence_rows, dpre)
        dnormed_two = lax.psum_scatter(
            contract_cols(dpre, up_full).astype(jnp.bfloat16),
            "mlp",
            scatter_dimension=0,
            tiled=True,
        ).astype(jnp.float32)
        dresid_norm, part_gain, part_shift = norm_back(
            dnormed_two, unit_two, scaled_two, second_gain
        )
        sum_second_gain = sum_second_gain + part_gain
        sum_second_shift = sum_second_shift + part_shift
        dresid = upstream + dresid_norm
        sum_attend_scale = sum_attend_scale + jnp.sum(attend * dresid, 0)
        dattend = attend_scale * dresid
        sum_outer_bias = sum_outer_bias + jnp.sum(dattend, 0)
        dattend_low = dattend.astype(jnp.bfloat16)
        sum_outer = sum_outer + contract_rows(mixed, dattend_low)
        dmixed = (
            contract_cols(dattend_low, outer_full)
            .astype(jnp.bfloat16)
            .reshape(rows, heads, head_dim)
        )
        logits = logits_of(query, keys, bias, allowed, factor)
        probs = jnp.exp(logits - log_total)
        dvalues = jnp.einsum(
            "hqk,qhd->khd", probs.astype(jnp.bfloat16), dmixed, preferred_element_type=jnp.float32
        )
        dprobs = jnp.einsum("qhd,khd->hqk", dmixed, values, preferred_element_type=jnp.float32)
        dlogits = probs * (dprobs - jnp.sum(dprobs * probs, -1, keepdims=True))
        sum_table_heads = sum_table_heads.at[:, flat_index].add(dlogits.reshape(heads, rows * rows))
        dlogits_low = dlogits.astype(jnp.bfloat16)
        dquery = (
            jnp.einsum("hqk,khd->qhd", dlogits_low, keys, preferred_element_type=jnp.float32)
            * factor
        )
        dkeys = (
            jnp.einsum("hqk,qhd->khd", dlogits_low, query, preferred_element_type=jnp.float32)
            * factor
        )
        dprojected = jnp.concatenate(
            [dquery.reshape(rows, width), dkeys.reshape(rows, width), dvalues.reshape(rows, width)],
            axis=1,
        ).astype(jnp.bfloat16)
        sum_query_bias = sum_query_bias + jnp.sum(dprojected[:, :width].astype(jnp.float32), 0)
        sum_value_bias = sum_value_bias + jnp.sum(dprojected[:, 2 * width :].astype(jnp.float32), 0)
        sum_inner = sum_inner + contract_rows(normed_one, dprojected)
        dnormed_one = contract_cols(dprojected, inner_full)
        dsource_norm, part_gain, part_shift = norm_back(
            dnormed_one, unit_one, scaled_one, first_gain
        )
        sum_first_gain = sum_first_gain + part_gain
        sum_first_shift = sum_first_shift + part_shift
        input_grads.append((dresid + dsource_norm).astype(jnp.bfloat16))
    sum_table = jnp.transpose(sum_table_heads)
    gradient_inner, gradient_outer = (
        lax.psum_scatter(sum_inner, ("dp", "mlp"), scatter_dimension=0, tiled=True),
        lax.psum_scatter(sum_outer, ("dp", "mlp"), scatter_dimension=0, tiled=True),
    )
    gradient_up, gradient_down = (
        lax.psum_scatter(sum_up, "dp", scatter_dimension=0, tiled=True),
        lax.psum_scatter(sum_down, "dp", scatter_dimension=1, tiled=True),
    )
    up_bias_full = lax.dynamic_update_slice_in_dim(
        jnp.zeros((up_bias.shape[0],), jnp.float32), sum_up_bias, col_start, 0
    )
    summed = lax.psum(
        (
            sum_first_gain,
            sum_first_shift,
            sum_query_bias,
            sum_value_bias,
            sum_outer_bias,
            sum_attend_scale,
            sum_second_gain,
            sum_second_shift,
            up_bias_full,
            sum_down_bias,
            sum_feed_scale,
            sum_table,
        ),
        ("dp", "mlp"),
    )
    return (
        jnp.stack(results),
        jnp.stack(input_grads),
        gradient_inner,
        gradient_outer,
        gradient_up,
        gradient_down,
        summed[0],
        summed[1],
        summed[2],
        summed[3],
        summed[4],
        summed[5],
        summed[6],
        summed[7],
        summed[8],
        summed[9],
        summed[10],
        summed[11],
    )


def solution(mesh):
    placed = (
        P(None, ("dp", "mlp"), None),
        P(None, ("dp", "mlp")),
        P(),
        P(None, ("dp", "mlp"), None),
        P(),
        P(),
        P(("dp", "mlp"), None),
        P(),
        P(),
        P(("dp", "mlp"), None),
        P(),
        P(),
        P(),
        P(),
        P("dp", "mlp"),
        P(),
        P("mlp", "dp"),
        P(),
        P(),
        P(),
    )
    return jax.shard_map(
        body,
        mesh=mesh,
        in_specs=placed,
        out_specs=(
            P(None, ("dp", "mlp"), None),
            P(None, ("dp", "mlp"), None),
            P(("dp", "mlp"), None),
            P(("dp", "mlp"), None),
            P("dp", "mlp"),
            P("mlp", "dp"),
            P(),
            P(),
            P(),
            P(),
            P(),
            P(),
            P(),
            P(),
            P(),
            P(),
            P(),
            P(),
        ),
        check_vma=False,
    )
```

profile of v0, /device:TPU:0, one launch (start us, length us, event | category | flops | bytes accessed | tf_op | source)
XLA Modules:
  0.0 1434.4 jit_solution(9241634660880689768)
XLA Ops:
  8.7 2.4 fusion.121
  14.9 129.0 %gather_fusion = f32[38809,12]{1,0:T(8,128)} fusion(f32[12,732]{0,1:T(8,128)S(1)} %bitcast.219, s32[38912]{0:T(1024)S(1)} %pad_clamp_fusion), kind=kCustom, calls=%fused_computation | custom fusion | bytes 3880900 | tf_op jit(solution)/shard_map/gather | solution.py:97
  143.9 11.1 copy.105
  154.9 2.8 reshape.322
  157.8 2.3 copy.106
  160.6 3.3 fusion.5
  170.5 3.0 fusion.4
  199.5 2.7 reshape.350
  202.2 2.7 reshape.348
  205.0 7.8 all-gather.23.cloned.1.call-done
  212.8 2.6 reshape.346
  215.5 16.5 %all-gather.21.cloned.1.call-done = bf16[4,197,768]{2,1,0:T(8,128)(2,1)} async-done(((bf16[1,197,768]{2,1,0:T(8,128)(2,1)}), bf16[4,197,768]{2,1,0:T(8,128)(2,1)}) %all-gather.21.cloned.1.call-update) | async-done | bytes 1210384 | tf_op jit(solution)/shard_map/all_gather | solution.py:148
  232.0 2.6 reshape.344
  234.6 40.6 %all-gather.17.cloned.1.call-done = bf16[768,768]{1,0:T(8,128)(2,1)} async-done(((bf16[96,768]{1,0:T(8,128)(2,1)}), bf16[768,768]{1,0:T(8,128)(2,1)}) %all-gather.17.cloned.1.call-update) | async-done | bytes 1179664 | tf_op jit(solution)/shard_map/all_gather | solution.py:42
  275.3 2.9 fusion.125
  279.6 3.5 multiply_convert_fusion.1
  283.2 34.1 %all-gather.19.cloned.1.call-done = bf16[768,768]{0,1:T(8,128)(2,1)} async-done(((bf16[768,96]{0,1:T(8,128)(2,1)}), bf16[768,768]{0,1:T(8,128)(2,1)}) %all-gather.19.cloned.1.call-update) | async-done | bytes 1179664 | tf_op jit(solution)/shard_map/all_gather | solution.py:43
  317.3 4.0 convolution_convert_fusion.2
  334.3 46.6 %fusion.114 = (bf16[200,768]{1,0:T(8,128)(2,1)}, bf16[200,768]{1,0:T(8,128)(2,1)}, bf16[200,768]{1,0:T(8,128)(2,1)}, bf16[200,768]{1,0:T(8,128)(2,1)}) fusion(bf16[788,768]{1,0:T(8,128)(2,1)} %convolution_convert_fusion.2, bf16[788,768]{1,0:T(8,128)(2,1)} %convolution_convert_fusion.3, bf16[788,768]{1,0:T(8,128)(2,1)} %convolution_convert_fusion, ...), kind=kCustom, calls=%all-reduce-scatter.4 | all-reduce-scatter fusion | flops 2457601 | bytes 6070784
  384.4 3.2 collective-permute-start.1
  393.2 4.0 concatenate.17
  399.9 4.0 concatenate.16
  404.0 4.0 concatenate.15
  408.0 3.4 fusion.82
  415.4 3.2 convolution_convert_fusion.4
  423.1 4.0 concatenate.14
  427.1 3.0 multiply_reduce_fusion.3
  441.0 3.4 copy.123
  449.0 4.7 fusion.74
  454.1 3.2 reshape.326
  457.3 9.7 copy.124
  467.0 2.8 reshape.334
  469.8 9.7 copy.126
  479.5 3.8 fusion.90
  490.5 207.4 %scatter_custom_fusion = f32[12,732]{0,1:T(8,128)S(1)} fusion(s32[38809]{0:T(1024)S(1)} %bitcast.254, f32[38809,12]{1,0:T(8,128)} %copy.124, f32[]{:T(128)} %constant.17.clone.1), kind=kCustom, calls=%fused_computation.189 | custom fusion | flops 465708 | bytes 35648 | tf_op jit(solution)/shard_map/scatter-add | solution.py:203
  697.9 207.6 %scatter_fusion = f32[12,732]{0,1:T(8,128)S(1)} fusion(f32[12,732]{0,1:T(8,128)S(1)} %scatter_custom_fusion, s32[38809]{0:T(1024)S(1)} %bitcast.255, f32[38809,12]{1,0:T(8,128)} %copy.126), kind=kCustom, calls=%fused_computation.2 | custom fusion | flops 465708 | bytes 5743732 | tf_op jit(solution)/shard_map/scatter-add | solution.py:203
  906.4 3.6 convolution_add_fusion.3
  910.2 3.3 fusion.126
  913.5 3.0 convolution_add_fusion.5
  916.6 3.3 fusion.127
  919.9 2.9 convolution_add_fusion.4
  924.0 2.4 fusion.91
  926.4 4.3 convolution_add_fusion
  934.8 102.6 %all-reduce.12.cloned.1.call-done = (f32[768]{0:T(1024)}, f32[768]{0:T(1024)}, f32[768]{0:T(1024)}, f32[768]{0:T(1024)}, f32[768]{0:T(1024)}, /*index=5*/f32[768...) async-done(((f32[768]{0:T(1024)}, f32[768]{0:T(1024)}, f32[768]{0:T(1024)}, ...) | async-done | bytes 78160 | tf_op jit(solution)/shard_map/psum | solution.py:239
  1039.1 104.1 %reduce-scatter.15.cloned.1.call-done = f32[24,768]{1,0:T(8,128)} async-done(((f32[768,768]{1,0:T(8,128)}), f32[24,768]{1,0:T(8,128)}) %reduce-scatter.15.cloned.1.call-update) | async-done | bytes 73744 | tf_op jit(solution)/shard_map/reduce_scatter | solution.py:230
  1143.3 72.6 %reduce-scatter.17.cloned.1.call-done = f32[96,768]{1,0:T(8,128)} async-done(((f32[768,768]{1,0:T(8,128)}), f32[96,768]{1,0:T(8,128)}) %reduce-scatter.17.cloned.1.call-update) | async-done | bytes 294928 | tf_op jit(solution)/shard_map/reduce_scatter | solution.py:233
  1215.8 72.4 %reduce-scatter.19.cloned.1.call-done = f32[768,96]{0,1:T(8,128)} async-done(((f32[768,768]{0,1:T(8,128)}), f32[768,96]{0,1:T(8,128)}) %reduce-scatter.19.cloned.1.call-update) | async-done | bytes 294928 | tf_op jit(solution)/shard_map/reduce_scatter | solution.py:234
  1288.3 125.4 %reduce-scatter.13.cloned.1.call-done = f32[24,2304]{1,0:T(8,128)} async-done(((f32[768,2304]{1,0:T(8,128)}), f32[24,2304]{1,0:T(8,128)}) %reduce-scatter.13.cloned.1.call-update) | async-done | bytes 221200 | tf_op jit(solution)/shard_map/reduce_scatter | solution.py:229
  (360 shorter events, 116.6 us)
Async XLA Ops:
  7.2 153.4 %all-gather.13.cloned.1.call-start = ((), (), s32[]{:S(2)}) async-start(), calls=%async_computation.4 | async-start | bytes 3649536 | tf_op jit(solution)/shard_map/all_gather | solution.py:38
  7.9 178.8 %all-gather.15.cloned.1.call-start = ((), (), s32[]{:S(2)}) async-start(), calls=%async_computation.5 | async-start | bytes 1216512 | tf_op jit(solution)/shard_map/all_gather | solution.py:39
  8.7 190.8 %all-gather.27.cloned.1.call-start = ((), (), s32[]{:S(2)}) async-start(), calls=%async_computation.15 | async-start | bytes 1536000 | tf_op jit(solution)/shard_map/all_gather | solution.py:169
  12.3 189.9 %all-gather.25.cloned.1.call-start = ((), (), s32[]{:S(2)}) async-start(), calls=%async_computation.14 | async-start | bytes 1536000 | tf_op jit(solution)/shard_map/all_gather | solution.py:169
  12.9 199.9 %all-gather.23.cloned.1.call-start = ((), (), s32[]{:S(2)}) async-start(), calls=%async_computation.13 | async-start | bytes 1536000 | tf_op jit(solution)/shard_map/all_gather | solution.py:148
  14.0 156.5 %copy-start.17 = (bf16[1,197,768]{2,1,0:T(8,128)(2,1)}, bf16[1,197,768]{2,1,0:T(8,128)(2,1)S(1)}, u32[]{:S(2)}) copy-start(bf16[1,197,768]{2,1,0:T(8,128)(2,1)S(1)} %get-tuple-element.179) | copy-start | bytes 907780
  14.3 146.3 %copy-start.72 = (f32[197]{0:T(256)}, f32[197]{0:T(256)S(1)}, u32[]{:S(2)}) copy-start(f32[197]{0:T(256)S(1)} %add_rsqrt_fusion.1) | copy-start | bytes 2368
  160.0 18.5 %copy-start.6 = (f32[197,197,12]{0,1,2:T(8,128)}, f32[197,197,12]{0,1,2:T(8,128)S(1)}, u32[]{:S(2)}) copy-start(f32[197,197,12]{0,1,2:T(8,128)S(1)} %copy.106) | copy-start | bytes 5588500
  160.1 10.4 copy-start.78
  160.3 10.2 copy-start.88
  176.5 6.6 copy-start.24
  192.2 39.8 %all-gather.21.cloned.1.call-start = ((), (), s32[]{:S(2)}) async-start(), calls=%async_computation.12 | async-start | bytes 1536000 | tf_op jit(solution)/shard_map/all_gather | solution.py:148
  192.8 82.5 %all-gather.17.cloned.1.call-start = ((), (), s32[]{:S(2)}) async-start(), calls=%async_computation.6 | async-start | bytes 1327104 | tf_op jit(solution)/shard_map/all_gather | solution.py:42
  193.5 123.8 %all-gather.19.cloned.1.call-start = ((), (), s32[]{:S(2)}) async-start(), calls=%async_computation.7 | async-start | bytes 1327104 | tf_op jit(solution)/shard_map/all_gather | solution.py:43
  194.3 843.0 %all-reduce.12.cloned.1.call-start = ((), (), s32[]{:S(2)}) async-start(), calls=%async_computation.16 | async-start | bytes 860160 | tf_op jit(solution)/shard_map/psum | solution.py:239
  199.4 5.5 copy-start.60
  199.4 5.5 copy-start.64
  199.4 5.5 copy-start.62
  199.5 5.5 copy-start.66
  275.3 4.4 copy-start.52
  275.3 4.4 copy-start.94
  334.3 63.0 %copy-start.77 = (f32[197]{0:T(256)S(1)}, f32[197]{0:T(256)}, u32[]{:S(2)}) copy-start(f32[197]{0:T(256)} %copy-done.76) | copy-start | bytes 2368
  334.3 63.0 %copy-start.87 = (f32[197]{0:T(256)S(1)}, f32[197]{0:T(256)}, u32[]{:S(2)}) copy-start(f32[197]{0:T(256)} %copy-done.86) | copy-start | bytes 2368
  380.9 27.1 %copy-start.71 = (f32[768]{0:T(1024)S(1)}, f32[768]{0:T(1024)}, u32[]{:S(2)}) copy-start(f32[768]{0:T(1024)} %param.38) | copy-start | bytes 9220
  380.9 27.1 %copy-start.75 = (f32[197]{0:T(256)S(1)}, f32[197]{0:T(256)}, u32[]{:S(2)}) copy-start(f32[197]{0:T(256)} %copy-done.74) | copy-start | bytes 2368
  380.9 27.1 %copy-start.81 = (f32[768]{0:T(1024)S(1)}, f32[768]{0:T(1024)}, u32[]{:S(2)}) copy-start(f32[768]{0:T(1024)} %param.37) | copy-start | bytes 9220
  380.9 27.1 %copy-start.84 = (f32[197]{0:T(256)S(1)}, f32[197]{0:T(256)}, u32[]{:S(2)}) copy-start(f32[197]{0:T(256)} %copy-done.83) | copy-start | bytes 2368
  381.7 18.2 %collective-permute-start.2 = (bf16[9,768]{1,0:T(8,128)(2,1)S(1)}, bf16[9,768]{1,0:T(8,128)(2,1)}, u32[]{:S(2)}, u32[]{:S(2)}) collective-permute-start(bf16[9,768]{1,0:T(8,128)(2,1)S(1)} %slice.62), channel_id=1, source_target_pairs={{0,1},{1,2},{2,3},{4,5},{5,6},{6,7},{8,9},{9,10},{10,11},{12,13},{... | collective-permute-start | bytes 41480
  384.4 19.6 %collective-permute-start.1 = (bf16[9,768]{1,0:T(8,128)(2,1)S(1)}, bf16[9,768]{1,0:T(8,128)(2,1)}, u32[]{:S(2)}, u32[]{:S(2)}) collective-permute-start(bf16[9,768]{1,0:T(8,128)(2,1)S(1)} %slice.61), channel_id=1, source_target_pairs={{0,1},{1,2},{2,3},{4,5},{5,6},{6,7},{8,9},{9,10},{10,11},{12,13},{... | collective-permute-start | bytes 41480
  388.3 4.9 collective-permute-start.3
  391.0 32.1 %collective-permute-start = (bf16[9,768]{1,0:T(8,128)(2,1)S(1)}, bf16[9,768]{1,0:T(8,128)(2,1)}, u32[]{:S(2)}, u32[]{:S(2)}) collective-permute-start(bf16[9,768]{1,0:T(8,128)(2,1)S(1)} %slice.60), channel_id=1, source_target_pairs={{0,1},{1,2},{2,3},{4,5},{5,6},{6,7},{8,9},{9,10},{10,11},{12,13},{... | collective-permute-start | bytes 41480
  393.2 18.2 %copy-start.69 = (f32[3072]{0:T(1024)}, f32[3072]{0:T(1024)S(1)}, u32[]{:S(2)}) copy-start(f32[3072]{0:T(1024)S(1)} %add_dynamic-update-slice_fusion) | copy-start | bytes 36868
  408.0 4.3 copy-start.9
  422.0 5.2 copy-start.82
  422.0 5.2 copy-start.85
  444.4 4.5 copy-start.19
  444.4 4.5 copy-start.79
  444.4 4.5 copy-start.89
  449.0 4.7 copy-start.32
  449.0 4.9 copy-start.30
  483.2 7.3 copy-start.34
  483.2 7.3 copy-start.54
  697.9 208.5 %copy-start.16 = (f32[197,768]{1,0:T(8,128)S(1)}, f32[197,768]{1,0:T(8,128)}, u32[]{:S(2)}) copy-start(f32[197,768]{1,0:T(8,128)} %copy-done.15) | copy-start | bytes 1815556
  697.9 208.5 %copy-start.43 = (bf16[12,64,197]{2,1,0:T(8,128)(2,1)S(1)}, bf16[12,64,197]{2,1,0:T(8,128)(2,1)}, u32[]{:S(2)}) copy-start(bf16[12,64,197]{2,1,0:T(8,128)(2,1)} %convolution_convert_fusion.6) | copy-start | bytes 907780
  906.3 236.9 %reduce-scatter.15.cloned.1.call-start = ((), (), s32[]{:S(2)}) async-start(), calls=%async_computation.9 | async-start | bytes 2433024 | tf_op jit(solution)/shard_map/reduce_scatter | solution.py:230
  910.0 305.9 %reduce-scatter.17.cloned.1.call-start = ((), (), s32[]{:S(2)}) async-start(), calls=%async_computation.10 | async-start | bytes 2654208 | tf_op jit(solution)/shard_map/reduce_scatter | solution.py:233
  916.5 371.7 %reduce-scatter.19.cloned.1.call-start = ((), (), s32[]{:S(2)}) async-start(), calls=%async_computation.11 | async-start | bytes 2654208 | tf_op jit(solution)/shard_map/reduce_scatter | solution.py:234
  922.9 490.8 %reduce-scatter.13.cloned.1.call-start = ((), (), s32[]{:S(2)}) async-start(), calls=%async_computation.8 | async-start | bytes 7299072 | tf_op jit(solution)/shard_map/reduce_scatter | solution.py:229
  (74 other events, 175.9 us)
Sparse Core Ops, SparseCore 0:
  10.9 62.8 all-gather.12
  76.7 52.8 all-gather.14
  131.2 16.6 all-gather.26
  149.3 17.7 all-gather.24
  192.3 20.4 all-gather.22
  214.2 17.7 all-gather.20
  234.2 41.0 all-gather.16
  277.4 39.8 all-gather.18
  906.5 130.8 all-reduce.11
  1043.0 100.1 reduce-scatter.14
  1147.7 68.0 reduce-scatter.16
  1220.2 68.0 reduce-scatter.18
  1295.5 118.1 reduce-scatter.12
where the time goes:
time: 1440 us; the launch traced here: 1430 us
  waiting for transfers between devices  580 us (40%)
  other arithmetic  441 us (31%)
  local copies, waits for them, and re-layouts  257 us (18%)
  matrix products  83.5 us (6%)
  blocking collectives  46.6 us (3%)
  between operations  16 us (1%)
    scatter-add x2, other arithmetic, body(): sum_table_heads.at[:, flat_index].add(dlogits.reshape(heads, rows * rows))  415 us
    gather x4, local copies, waits for them, and re-layouts, body(): bias = table_by_head[:, position_index]  145 us
    reduce_scatter x1, waiting for transfers between devices, body(): lax.psum_scatter(sum_inner, ('dp', 'mlp'), scatter_dimension=0, tiled=True)  125 us
    reduce_scatter x1, waiting for transfers between devices, body(): lax.psum_scatter(sum_outer, ('dp', 'mlp'), scatter_dimension=0, tiled=True)  104 us
    psum x1, waiting for transfers between devices, body(): lax.psum((sum_first_gain, sum_first_shift, sum_query_bias, sum_value_bias...  103 us
    reduce_scatter x1, waiting for transfers between devices, body(): lax.psum_scatter(sum_up, 'dp', scatter_dimension=0, tiled=True)  72.6 us
    reduce_scatter x1, waiting for transfers between devices, body(): lax.psum_scatter(sum_down, 'dp', scatter_dimension=1, tiled=True)  72.4 us
    unnamed x238, local copies, waits for them, and re-layouts  60.9 us
  transfers between devices with their start and end apart: 17, of which 9 were waited for; matrix products, arithmetic and copies ran while one was open for 18% of the time, Pallas kernels for 0%

commit v1 on v0

--- a/solution.py
+++ b/solution.py
@@ -1,11 +1,312 @@
 import jax
 import jax.numpy as jnp
 from jax import lax
+from jax.experimental import pallas as pl
+from jax.experimental.pallas import tpu as pltpu
 from jax.sharding import PartitionSpec as P
 
 EPS = 1e-06
 ROOT_HALF = 0.7071067811865476
 DENSITY = 0.3989422804014327
+
+
+MESH = pl.DeviceIdType.MESH
+KINDS = (0, 0, 0, 0, 1, 1, 1, 1)
+SLOT = (0, 1, 2, 3, 0, 1, 2, 3)
+Y_LAST = (True, False, True, False, True, False, True, False)
+N_COPY = 10
+
+
+def place():
+    dp = lax.axis_index("dp")
+    mlp = lax.axis_index("mlp")
+    return lax.div(dp, 2), lax.rem(dp, 2), lax.div(mlp, 2), lax.rem(mlp, 2)
+
+
+def device(z, x, y, c):
+    return (z * 2 + x, y * 2 + c)
+
+
+def own(ref, kind, z, x, y, c):
+    return ref.at[c, z, x, y] if kind == 0 else ref.at[y, c, z, x]
+
+
+def line(ref, kind, x, y, c):
+    return ref.at[c, :, x, y] if kind == 0 else ref.at[y, c, :, x]
+
+
+def greet(z, x, y, c):
+    barrier = pltpu.get_barrier_semaphore()
+    others = [device(lax.rem(z + d, 4), x, y, c) for d in (1, 2, 3)]
+    others += [device(z, 1 - x, y, c), device(z, x, 1 - y, c), device(z, x, y, 1 - c)]
+    for other in others:
+        pl.semaphore_signal(barrier, inc=1, device_id=other, device_id_type=MESH)
+    pl.semaphore_wait(barrier, len(others))
+
+
+class Link:
+    def __init__(self, send, recv):
+        self.send, self.recv, self.pending = send, recv, []
+
+    def copy(self, src, dst, slot, target):
+        made = pltpu.make_async_remote_copy(
+            src_ref=src,
+            dst_ref=dst,
+            send_sem=self.send.at[slot],
+            recv_sem=self.recv.at[slot],
+            device_id=target,
+            device_id_type=MESH,
+        )
+        made.start()
+        self.pending.append(made)
+        return made
+
+    def drain(self):
+        for made in self.pending:
+            made.wait_send()
+        self.pending = []
+
+
+class Gather:
+    def __init__(self, link, ref, unit, where):
+        self.link, self.ref, self.unit, self.where = link, ref, unit, where
+        self.kind = KINDS[unit]
+        self.base = unit * N_COPY
+        self.y_last = Y_LAST[unit]
+
+    def put(self, part, slot, target):
+        return self.link.copy(part, part, self.base + slot, target)
+
+    def along_z(self):
+        z, x, y, c = self.where
+        part = own(self.ref, self.kind, z, x, y, c)
+        self.z = [self.put(part, d - 1, device(lax.rem(z + d, 4), x, y, c)) for d in (1, 2, 3)]
+
+    def line_out(self):
+        z, x, y, c = self.where
+        for made in self.z:
+            made.wait_recv()
+        part = line(self.ref, self.kind, x, y, c)
+        self.to_x = self.put(part, 3, device(z, 1 - x, y, c))
+        self.to_y = self.put(part, 4, device(z, x, 1 - y, c))
+        self.to_c = [self.put(part, 6, device(z, x, y, 1 - c))]
+
+    def plane_out(self):
+        z, x, y, c = self.where
+        mirror = device(z, x, y, 1 - c)
+        if self.y_last:
+            self.to_x.wait_recv()
+            part = line(self.ref, self.kind, 1 - x, y, c)
+            self.last = self.put(part, 5, device(z, x, 1 - y, c))
+            self.to_c.append(self.put(part, 7, mirror))
+            self.to_y.wait_recv()
+            self.to_c.append(self.put(line(self.ref, self.kind, x, 1 - y, c), 8, mirror))
+        else:
+            self.to_y.wait_recv()
+            part = line(self.ref, self.kind, x, 1 - y, c)
+            self.last = self.put(part, 5, device(z, 1 - x, y, c))
+            self.to_c.append(self.put(part, 7, mirror))
+            self.to_x.wait_recv()
+            self.to_c.append(self.put(line(self.ref, self.kind, 1 - x, y, c), 8, mirror))
+
+    def core_out(self):
+        z, x, y, c = self.where
+        self.last.wait_recv()
+        part = line(self.ref, self.kind, 1 - x, 1 - y, c)
+        self.to_c.append(self.put(part, 9, device(z, x, y, 1 - c)))
+
+    def finish(self):
+        for made in self.to_c:
+            made.wait_recv()
+
+
+def gather_kernel(small_ref, large_ref, narrow_ref, wide_ref, pair, send, recv):
+    where = z, x, y, c = place()
+    greet(*where)
+    link = Link(send, recv)
+    pair[:, c] = small_ref[:, c]
+    mate = link.copy(small_ref.at[:, 1 - c], pair.at[:, c], 8 * N_COPY, device(z, x, y, 1 - c))
+    for unit in range(4):
+        wide_ref[unit, y, c, z, x] = large_ref[unit]
+    mate.wait_recv()
+    for unit in range(4):
+        narrow_ref[unit, c, z, x, y] = pair[unit].reshape(48, 384).astype(jnp.bfloat16)
+    units = [Gather(link, (narrow_ref if KINDS[u] == 0 else wide_ref).at[SLOT[u]], u, where) for u in range(8)]
+    for unit in units:
+        unit.along_z()
+    for step in range(8 + 2):
+        if step < 8:
+            units[step].line_out()
+        if 0 <= step - 1 < 8:
+            units[step - 1].plane_out()
+        if 0 <= step - 2 < 8:
+            units[step - 2].core_out()
+    for unit in units:
+        unit.finish()
+    link.drain()
+
+
+def gather_all(small, large):
+    return pl.pallas_call(
+        gather_kernel,
+        out_shape=(
+            jax.ShapeDtypeStruct((4, 2, 4, 2, 2, 48, 384), jnp.bfloat16),
+            jax.ShapeDtypeStruct((4, 2, 2, 4, 2, 96, 384), jnp.bfloat16),
+        ),
+        in_specs=[pl.BlockSpec(memory_space=pltpu.VMEM)] * 2,
+        out_specs=[pl.BlockSpec(memory_space=pltpu.VMEM)] * 2,
+        scratch_shapes=[
+            pltpu.VMEM((4, 2, 24, 384), jnp.float32),
+            pltpu.SemaphoreType.DMA((8 * N_COPY + 1,)),
+            pltpu.SemaphoreType.DMA((8 * N_COPY + 1,)),
+        ],
+        compiler_params=pltpu.CompilerParams(
+            collective_id=0, has_side_effects=True, vmem_limit_bytes=56 * 2**20
+        ),
+    )(small, large)
+
+
+class Scatter:
+    def __init__(self, link, ref, half, quarter, eighth, parts, unit, where):
+        self.link, self.ref, self.unit, self.where = link, ref, unit, where
+        self.half, self.quarter, self.eighth, self.parts = half, quarter, eighth, parts
+        self.kind = KINDS[unit]
+        self.base = unit * N_COPY
+        self.x_last = Y_LAST[unit]
+
+    def put(self, src, dst, slot, target):
+        return self.link.copy(src, dst, self.base + slot, target)
+
+    def by_core(self, ref, c):
+        return ref.at[c] if self.kind == 0 else ref.at[:, c]
+
+    def by_y(self, ref, y, c):
+        return ref.at[c, :, :, y] if self.kind == 0 else ref.at[y, c]
+
+    def by_x(self, ref, x, c):
+        return ref.at[c, :, x] if self.kind == 0 else ref.at[:, c, :, x]
+
+    def mix(self, here, there):
+        total = here[...].astype(jnp.float32) + there[...].astype(jnp.float32)
+        here[...] = total.astype(jnp.bfloat16)
+
+    def to_core(self):
+        z, x, y, c = self.where
+        self.made = self.put(self.by_core(self.ref, 1 - c), self.half, 0, device(z, x, y, 1 - c))
+
+    def to_first(self):
+        z, x, y, c = self.where
+        self.made.wait_recv()
+        self.mix(self.by_core(self.ref, c), self.half)
+        if self.x_last:
+            self.made = self.put(self.by_y(self.ref, 1 - y, c), self.quarter, 1, device(z, x, 1 - y, c))
+        else:
+            self.made = self.put(self.by_x(self.ref, 1 - x, c), self.quarter, 1, device(z, 1 - x, y, c))
+
+    def to_second(self):
+        z, x, y, c = self.where
+        self.made.wait_recv()
+        self.mix(self.by_y(self.ref, y, c) if self.x_last else self.by_x(self.ref, x, c), self.quarter)
+        if self.x_last:
+            self.made = self.put(line(self.ref, self.kind, 1 - x, y, c), self.eighth, 2, device(z, 1 - x, y, c))
+        else:
+            self.made = self.put(line(self.ref, self.kind, x, 1 - y, c), self.eighth, 2, device(z, x, 1 - y, c))
+
+    def to_z(self):
+        z, x, y, c = self.where
+        self.made.wait_recv()
+        self.mix(line(self.ref, self.kind, x, y, c), self.eighth)
+        self.z = []
+        for d in (1, 2, 3):
+            far = lax.rem(z + d, 4)
+            src = own(self.ref, self.kind, far, x, y, c)
+            self.z.append(self.put(src, self.parts.at[d - 1], 2 + d, device(far, x, y, c)))
+
+    def total(self):
+        for made in self.z:
+            made.wait_recv()
+        total = own(self.ref, self.kind, *self.where)[...].astype(jnp.float32)
+        for d in range(3):
+            total = total + self.parts[d].astype(jnp.float32)
+        return total
+
+
+def reduce_kernel(narrow_in, wide_in, small_ref, large_ref, narrow_ref, wide_ref, half0, half1, quarter0, quarter1a, quarter1b, eighth0, eighth1, parts0, parts1, mine, send, recv, local):
+    where = z, x, y, c = place()
+    greet(*where)
+    link = Link(send, recv)
+    bring = [
+        pltpu.make_async_copy(narrow_in, narrow_ref, local.at[0]),
+        pltpu.make_async_copy(wide_in, wide_ref, local.at[1]),
+    ]
+    for made in bring:
+        made.start()
+    for made in bring:
+        made.wait()
+    units = []
+    for u in range(8):
+        s = SLOT[u]
+        if KINDS[u] == 0:
+            units.append(Scatter(link, narrow_ref.at[s], half0.at[s], quarter0.at[s], eighth0.at[s], parts0.at[s], u, where))
+        else:
+            quarter1 = quarter1a if Y_LAST[u] else quarter1b
+            units.append(Scatter(link, wide_ref.at[s], half1.at[s], quarter1.at[s // 2], eighth1.at[s], parts1.at[s], u, where))
+    for unit in units:
+        unit.to_core()
+    mates = []
+    for step in range(8 + 3):
+        if step < 8:
+            units[step].to_first()
+        if 0 <= step - 1 < 8:
+            units[step - 1].to_second()
+        if 0 <= step - 2 < 8:
+            units[step - 2].to_z()
+        u = step - 3
+        if 0 <= u < 8:
+            total = units[u].total()
+            if KINDS[u] == 0:
+                s = SLOT[u]
+                mine[s] = total.reshape(2, 24, 384)
+                small_ref[s, c] = mine[s, c]
+                mates.append(link.copy(mine.at[s, 1 - c], small_ref.at[s, c], 8 * N_COPY + s, device(z, x, y, 1 - c)))
+            else:
+                large_ref[SLOT[u]] = total
+    for made in mates:
+        made.wait_recv()
+    link.drain()
+
+
+def reduce_all(narrow, wide):
+    bf = jnp.bfloat16
+    return pl.pallas_call(
+        reduce_kernel,
+        out_shape=(
+            jax.ShapeDtypeStruct((4, 2, 24, 384), jnp.float32),
+            jax.ShapeDtypeStruct((4, 96, 384), jnp.float32),
+        ),
+        in_specs=[pl.BlockSpec(memory_space=pl.ANY)] * 2,
+        out_specs=[pl.BlockSpec(memory_space=pltpu.VMEM)] * 2,
+        scratch_shapes=[
+            pltpu.VMEM((4, 2, 4, 2, 2, 48, 384), bf),
+            pltpu.VMEM((4, 2, 2, 4, 2, 96, 384), bf),
+            pltpu.VMEM((4, 4, 2, 2, 48, 384), bf),
+            pltpu.VMEM((4, 2, 4, 2, 96, 384), bf),
+            pltpu.VMEM((4, 4, 2, 48, 384), bf),
+            pltpu.VMEM((2, 4, 2, 96, 384), bf),
+            pltpu.VMEM((2, 2, 4, 96, 384), bf),
+            pltpu.VMEM((4, 4, 48, 384), bf),
+            pltpu.VMEM((4, 4, 96, 384), bf),
+            pltpu.VMEM((4, 3, 48, 384), bf),
+            pltpu.VMEM((4, 3, 96, 384), bf),
+            pltpu.VMEM((4, 2, 24, 384), jnp.float32),
+            pltpu.SemaphoreType.DMA((8 * N_COPY + 4,)),
+            pltpu.SemaphoreType.DMA((8 * N_COPY + 4,)),
+            pltpu.SemaphoreType.DMA((2,)),
+        ],
+        compiler_params=pltpu.CompilerParams(
+            collective_id=1, has_side_effects=True, vmem_limit_bytes=56 * 2**20
+        ),
+    )(narrow, wide)
 
 
 def layer_norm(values, gain, shift):
@@ -275,7 +576,124 @@
     )
 
 
+def fast_body(
+    tokens, keep_mask, position_index, cotangent, first_gain, first_shift, inner_weight, query_bias,
+    value_bias, outer_weight, outer_bias, attend_scale, second_gain, second_shift, up_weight, up_bias,
+    down_weight, down_bias, feed_scale, position_table,
+):
+    micro, rows, width = tokens.shape
+    heads = position_table.shape[1]
+    head_dim = width // heads
+    factor = head_dim ** (-0.5)
+    f32, bf = jnp.float32, jnp.bfloat16
+    inner_piece = inner_weight.reshape(24, 3, 2, 3, 128).transpose(3, 2, 0, 1, 4).reshape(3, 2, 24, 384)
+    outer_piece = outer_weight.reshape(24, 2, 384).transpose(1, 0, 2)[None]
+    small = jnp.concatenate([inner_piece, outer_piece]).astype(f32)
+    large = jnp.concatenate(
+        [up_weight.reshape(96, 2, 384).transpose(1, 0, 2), down_weight.T.reshape(96, 2, 384).transpose(1, 0, 2)]
+    )
+    narrow, wide = gather_all(small, large)
+    narrow = narrow.reshape(4, 2, 768, 384)
+    inner_full = narrow[:3].reshape(3, 2, 768, 3, 128).transpose(2, 3, 1, 0, 4).reshape(768, 2304)
+    outer_full = narrow[3].transpose(1, 0, 2).reshape(768, 768)
+    wide = wide.reshape(2, 2, 2, 2, 768, 384)
+    up_full = wide[0].transpose(3, 1, 2, 0, 4).reshape(768, 3072)
+    down_full = wide[1].transpose(3, 1, 2, 0, 4).reshape(768, 3072)
+    shift_vector = jnp.concatenate([query_bias, jnp.zeros_like(query_bias), value_bias])
+    one_hot = (position_index.reshape(1, rows * rows) == lax.broadcasted_iota(jnp.int32, (position_table.shape[0], 1), 0))
+    high = position_table.astype(bf)
+    rest = (position_table - high.astype(f32)).astype(bf)
+    hot = one_hot.astype(bf)
+    bias = contract_rows(high, hot) + contract_rows(rest, hot)
+    bias = bias.reshape(heads, rows, rows)
+    seen = jnp.arange(rows)
+    diagonal = seen[:, None] == seen[None, :]
+    source = tokens.astype(f32)
+    allowed = jnp.logical_or(keep_mask[:, None, None, :] == 1, diagonal[None, None])
+    normed_one, unit_one, scaled_one = layer_norm(source, first_gain, first_shift)
+    normed_one = normed_one.astype(bf).reshape(micro * rows, width)
+    projected = (jnp.dot(normed_one, inner_full, preferred_element_type=f32) + shift_vector).astype(bf)
+    split = projected.reshape(micro, rows, 3, heads, head_dim).transpose(2, 0, 3, 1, 4)
+    query, keys, values = split[0], split[1], split[2]
+    logits = jnp.einsum("bhqd,bhkd->bhqk", query, keys, preferred_element_type=f32) * factor + bias[None]
+    logits = jnp.where(allowed, logits, -1e30)
+    top = jnp.max(logits, -1, keepdims=True)
+    expd = jnp.exp(logits - top)
+    probs = expd / jnp.sum(expd, -1, keepdims=True)
+    probs_low = probs.astype(bf)
+    mixed = jnp.einsum("bhqk,bhkd->bhqd", probs_low, values, preferred_element_type=f32)
+    mixed = mixed.transpose(0, 2, 1, 3).reshape(micro * rows, width).astype(bf)
+    attend = jnp.dot(mixed, outer_full, preferred_element_type=f32) + outer_bias
+    flat = source.reshape(micro * rows, width)
+    resid = flat + attend_scale * attend
+    normed_two, unit_two, scaled_two = layer_norm(resid, second_gain, second_shift)
+    normed_two = normed_two.astype(bf)
+    pre = jnp.dot(normed_two, up_full, preferred_element_type=f32) + up_bias
+    active, slope = gelu_pair(pre)
+    hidden = active.astype(bf)
+    feed = contract_cols(hidden, down_full) + down_bias
+    result = (resid + feed_scale * feed).astype(bf).reshape(micro, rows, width)
+    upstream = cotangent.astype(f32).reshape(micro * rows, width)
+    sum_feed_scale = jnp.sum(feed * upstream, 0)
+    dfeed = feed_scale * upstream
+    sum_down_bias = jnp.sum(dfeed, 0)
+    dfeed_low = dfeed.astype(bf)
+    grad_down = contract_rows(dfeed_low, hidden)
+    dpre = (jnp.dot(dfeed_low, down_full, preferred_element_type=f32) * slope).astype(bf)
+    sum_up_bias = jnp.sum(dpre.astype(f32), 0)
+    grad_up = contract_rows(normed_two, dpre)
+    dnormed_two = contract_cols(dpre, up_full)
+    dresid_norm, sum_second_gain, sum_second_shift = norm_back(dnormed_two, unit_two, scaled_two, second_gain)
+    dresid = upstream + dresid_norm
+    sum_attend_scale = jnp.sum(attend * dresid, 0)
+    dattend = attend_scale * dresid
+    sum_outer_bias = jnp.sum(dattend, 0)
+    dattend_low = dattend.astype(bf)
+    grad_outer = contract_rows(mixed, dattend_low)
+    dmixed = contract_cols(dattend_low, outer_full).astype(bf)
+    dmixed = dmixed.reshape(micro, rows, heads, head_dim).transpose(0, 2, 1, 3)
+    dvalues = jnp.einsum("bhqk,bhqd->bhkd", probs_low, dmixed, preferred_element_type=f32)
+    dprobs = jnp.einsum("bhqd,bhkd->bhqk", dmixed, values, preferred_element_type=f32)
+    dlogits = probs * (dprobs - jnp.sum(dprobs * probs, -1, keepdims=True))
+    summed_logits = jnp.sum(dlogits, 0).reshape(heads, rows * rows)
+    part = summed_logits.astype(bf)
+    part2 = (summed_logits - part.astype(f32)).astype(bf)
+    sum_table = contract_cols(hot, part) + contract_cols(hot, part2)
+    dlogits_low = dlogits.astype(bf)
+    dquery = jnp.einsum("bhqk,bhkd->bhqd", dlogits_low, keys, preferred_element_type=f32) * factor
+    dkeys = jnp.einsum("bhqk,bhqd->bhkd", dlogits_low, query, preferred_element_type=f32) * factor
+    dprojected = jnp.stack([dquery, dkeys, dvalues]).astype(bf).transpose(1, 3, 0, 2, 4).reshape(micro * rows, 3 * width)
+    sum_query_bias = jnp.sum(dprojected[:, :width].astype(f32), 0)
+    sum_value_bias = jnp.sum(dprojected[:, 2 * width :].astype(f32), 0)
+    grad_inner = contract_rows(normed_one, dprojected)
+    dnormed_one = contract_cols(dprojected, inner_full)
+    dsource, sum_first_gain, sum_first_shift = norm_back(
+        dnormed_one, unit_one.reshape(micro * rows, width), scaled_one.reshape(micro * rows, 1), first_gain
+    )
+    input_grad = (dresid + dsource).astype(bf).reshape(micro, rows, width)
+    narrow_grad = jnp.concatenate(
+        [
+            grad_inner.astype(bf).reshape(768, 3, 2, 3, 128).transpose(3, 2, 0, 1, 4).reshape(3, 2, 768, 384),
+            grad_outer.astype(bf).reshape(768, 2, 384).transpose(1, 0, 2)[None],
+        ]
+    ).reshape(4, 2, 4, 2, 2, 48, 384)
+    wide_grad = jnp.stack([grad_up, grad_down]).astype(bf).reshape(2, 768, 2, 2, 2, 384)
+    wide_grad = wide_grad.transpose(0, 4, 2, 3, 1, 5).reshape(4, 2, 2, 4, 2, 96, 384)
+    small_out, large_out = reduce_all(narrow_grad, wide_grad)
+    gradient_inner = small_out[:3].reshape(3, 2, 24, 3, 128).transpose(2, 3, 1, 0, 4).reshape(24, 2304)
+    gradient_outer = small_out[3].transpose(1, 0, 2).reshape(24, 768)
+    gradient_up = large_out[:2].transpose(1, 0, 2).reshape(96, 768)
+    gradient_down = large_out[2:].transpose(1, 0, 2).reshape(96, 768).T
+    vectors = [
+        sum_first_gain, sum_first_shift, sum_query_bias, sum_value_bias, sum_outer_bias, sum_attend_scale,
+        sum_second_gain, sum_second_shift, sum_up_bias, sum_down_bias, sum_feed_scale,
+    ]
+    summed = lax.psum((*vectors, sum_table), ("dp", "mlp"))
+    return (result, input_grad, gradient_inner, gradient_outer, gradient_up, gradient_down, *summed)
+
+
 def solution(mesh):
+    special = mesh.shape["dp"] == 8 and mesh.shape["mlp"] == 4
     placed = (
         P(None, ("dp", "mlp"), None),
         P(None, ("dp", "mlp")),
@@ -299,7 +717,7 @@
         P(),
     )
     return jax.shard_map(
-        body,
+        fast_body if special else body,
         mesh=mesh,
         in_specs=placed,
         out_specs=(

time: 1440 us -> 588 us (0.41)
  waiting for transfers between devices: 580 us -> 0.02 us
  other arithmetic: 441 us -> 40.3 us
  Pallas kernels: 0 us -> 175 us
  matrix products: 83.5 us -> 165 us
  local copies, waits for them, and re-layouts: 257 us -> 183 us
  blocking collectives: 46.6 us -> 0 us
    scatter-add x2 -> x0, other arithmetic: 415 us -> none  [body(): sum_table_heads.at[:, flat_index].add(dlogits.reshape(heads, rows * rows))]
    reduce_scatter x4 -> x0, waiting for transfers between devices: 375 us -> none  [the longest x1 125 us: body(): lax.psum_scatter(sum_inner, ('dp', 'mlp'), scatter_dimension=0, tiled=True)]
    pallas_call x0 -> x2, Pallas kernels: none -> 175 us  [the longest x1 91.9 us: reduce_all(): pl.pallas_call(reduce_kernel, out_shape=(jax.ShapeDtypeStruct((4, 2, 24,...]
    gather x4 -> x0, local copies, waits for them, and re-layouts: 145 us -> none  [body(): bias = table_by_head[:, position_index]]
    psum x1, waiting for transfers between devices: 103 us -> 0.01 us  [fast_body(): summed = lax.psum((*vectors, sum_table), ('dp', 'mlp'))]
    all_gather x8 -> x0, waiting for transfers between devices: 99.2 us -> none  [the longest x1 40.6 us: fetch(): lax.all_gather(up_weight, 'dp', axis=0, tiled=True)]
    unnamed x1 -> x0, blocking collectives: 46.6 us -> none
    dot_general x8 -> x6, matrix products: 20 us -> 63 us  [contract_cols(): lax.dot_general(left, right, (((1,), (1,)), ((), ())), preferred_element_...]
  transfers between devices with their start and end apart: 17 -> 1, of which waited for: 9 -> 0; matrix products, arithmetic and copies ran while one was open for 18% -> 16% of each run, Pallas kernels for 0% -> 16%
where the time goes in v1:
time: 588 us; the launch traced here: 579 us
  local copies, waits for them, and re-layouts  183 us (31%)
  Pallas kernels  175 us (30%)
  matrix products  165 us (28%)
  other arithmetic  40.3 us (7%)
  between operations  14.9 us (3%)
    pallas_call x1, Pallas kernels, reduce_all(): pl.pallas_call(reduce_kernel, out_shape=(jax.ShapeDtypeStruct((4, 2, 24,...  91.9 us
    pallas_call x1, Pallas kernels, gather_all(): pl.pallas_call(gather_kernel, out_shape=(jax.ShapeDtypeStruct((4, 2, 4, 2...  83.5 us
    dot_general x6, matrix products, contract_cols(): lax.dot_general(left, right, (((1,), (1,)), ((), ())), preferred_element_...  63 us
    dot_general x6, matrix products, contract_rows(): lax.dot_general(left, right, (((0,), (0,)), ((), ())), preferred_element_...  58.7 us
    unnamed x115, local copies, waits for them, and re-layouts  24.9 us
    dot_general x1, matrix products, fast_body(): jnp.dot(dfeed_low, down_full, preferred_element_type=f32) * slope  18.1 us
    another operation x2, local copies, waits for them, and re-layouts, fast_body(): jnp.stack([grad_up, grad_down]).astype(bf).reshape(2, 768, 2, 2, 2, 384)  16.9 us
    reshape x2, local copies, waits for them, and re-layouts, fast_body(): projected.reshape(micro, rows, 3, heads, head_dim).transpose(2, 0, 3, 1, 4)  12.3 us
  transfers between devices with their start and end apart: 1, of which 0 were waited for; matrix products, arithmetic and copies ran while one was open for 16% of the time, Pallas kernels for 16%

profile of v1, /device:TPU:0, one launch (start us, length us, event | category | flops | bytes accessed | tf_op | source)
XLA Modules:
  0.0 578.9 jit_solution(8584789717898818353)
XLA Ops:
  12.3 83.5 %shard_map.331 = (bf16[4,2,4,2,2,48,384]{6,5,4,3,2,1,0:T(8,128)(2,1)}, bf16[4,2,2,4,2,96,384]{6,5,4,3,2,1,0:T(8,128)(2,1)}) custom-call(f32[4,2,24,384]{3,2,1,0:T(8,128)} %maximum_convert_fusion.small_ref, bf16[4,96,384]{2,1,0:T(8,128)(2,1)} %pad_maximum_fusion.1.large_ref), custom_call_target="tpu_custom_call" | custom-call | tf_op jit(solution)/shard_map/pallas_call | solution.py:150
  98.2 2.5 slice.47
  103.0 5.2 reshape.262
  108.2 6.5 %copy.183 = bf16[768,3,2,3,128]{0,4,3,2,1:T(8,128)(2,1)S(1)} copy(bf16[768,3,2,3,128]{4,1,0,2,3:T(4,128)(2,1)} %bitcast.146) | data formatting | bytes 7077888 | tf_op jit(solution)/shard_map/transpose | solution.py:597
  115.8 2.4 multiply_reduce_fusion.8
  118.3 3.1 subtract_multiply_fusion.2
  124.3 4.0 fusion.21
  128.3 6.6 %reshape.284 = bf16[2,197,3,12,64]{4,3,2,1,0:T(8,128)(2,1)} reshape(bf16[394,2304]{1,0:T(8,128)(2,1)} %fusion.21) | data formatting | bytes 3631104 | tf_op jit(solution)/shard_map/reshape | solution.py:616
  134.9 5.7 copy.185
  140.7 3.2 fusion.39
  144.2 19.6 %fusion.3 = f32[12,38809]{1,0:T(8,128)S(1)} fusion(s32[38809]{0:T(1024)S(1)} %eq.44, f32[732,12]{0,1:T(8,128)S(1)} %copy-done.39), kind=kOutput, calls=%fused_computation.4 | convolution fusion | flops 710239808 | bytes 2053204 | tf_op jit(solution)/shard_map/dot_general | solution.py:350
  163.8 18.8 %fusion.10 = f32[12,38809]{1,0:T(8,128)} fusion(f32[12,38809]{1,0:T(8,128)S(1)} %fusion.3, s32[38809]{0:T(1024)S(1)} %eq.44, f32[732,12]{0,1:T(8,128)S(1)} %copy-done.39), kind=kOutput, calls=%fused_computation.11 | convolution fusion | flops 710679168 | bytes 3916036 | tf_op jit(solution)/shard_map/dot_general | solution.py:350
  182.7 4.1 add.152
  186.7 3.6 copy.186
  190.5 7.5 %fusion.52 = (f32[2,12,197]{2,1,0:T(8,128)S(1)}, f32[2,12,197,197]{2,3,1,0:T(8,128)S(1)}) fusion(f32[2,12,197,197]{2,3,1,0:T(8,128)} %fusion.39, f32[12,197,197]{1,2,0:T(8,128)} %copy.186, pred[2,197,197]{1,2,0:T(8,128)(4,1)S(1)} %broadcast_or_fusion), kind=kOutput, calls=%fused_computation.129 | output fusion | flops 7451524 | bytes 9410690 | tf_op jit(solution)/shard_map/sub | solution.py:621
  204.0 2.4 reshape.255
  206.5 3.4 fusion.50
  211.8 8.7 %fusion.51 = (bf16[2,2,2,4,2,96,384]{6,5,4,3,2,1,0:T(8,128)(2,1)}, bf16[2,2,2,4,2,96,384]{6,5,4,3,2,1,0:T(8,128)(2,1)}) fusion(bf16[4,2,2,4,2,96,384]{6,5,4,3,2,1,0:T(8,128)(2,1)} %get-tuple-element.23), kind=kLoop, calls=%fused_computation.128 | loop fusion | bytes 18874368 | tf_op jit(solution)/shard_map/slice | solution.py:600
  220.5 6.6 %copy.190 = bf16[2,2,2,768,384]{3,4,0,2,1:T(8,128)(2,1)} copy(bf16[2,2,2,768,384]{4,3,2,1,0:T(8,128)(2,1)} %bitcast.145) | data formatting | bytes 9437184 | tf_op jit(solution)/shard_map/squeeze | solution.py:600
  227.2 6.7 %copy.191 = bf16[2,2,2,768,384]{3,4,0,2,1:T(8,128)(2,1)} copy(bf16[2,2,2,768,384]{4,3,2,1,0:T(8,128)(2,1)} %bitcast.144) | data formatting | bytes 9437184 | tf_op jit(solution)/shard_map/squeeze | solution.py:601
  236.1 2.5 multiply_reduce_fusion.12
  241.6 5.9 %fusion.20 = (bf16[3072,394]{0,1:T(8,128)(2,1)}, f32[394,3072]{1,0:T(8,128)S(1)}) fusion(f32[3072]{0:T(1024)} %param.35, bf16[768,3072]{0,1:T(8,128)(2,1)} %bitcast.160, f32[394,768]{1,0:T(8,128)} %copy-done.6, f32[768]{0:T(1024)} %param.33, f32[768]{0:T(1024)} %param.32, f32[394]{0:T(512)} %add_rsqrt_fusion.1, f32[394]{0:T(512)S(1)} %broadcast_multiply_fusion.5), kind=kOutput, calls=%fused_computation.34 | convolution fusion | flops 1867900416 | bytes 13212752 | tf_op jit(solution)/shard_map/dot_general | solution.py:631
  247.6 18.1 %convert_reduce_fusion = (f32[3072]{0:T(1024)}, bf16[394,3072]{1,0:T(8,128)(2,1)S(1)}) fusion(f32[394,3072]{1,0:T(8,128)S(1)} %get-tuple-element.163, bf16[394,768]{1,0:T(8,128)(2,1)S(1)} %copy-done.21, bf16[768,3072]{0,1:T(8,128)(2,1)} %bitcast.158), kind=kOutput, calls=%fused_computation.27 | convolution fusion | flops 1873646592 | bytes 12598272 | tf_op jit(solution)/shard_map/dot_general | solution.py:642
  265.7 3.9 multiply_reduce_fusion.2
  270.8 2.4 reshape.269
  273.2 8.3 %multiply_reduce_fusion.3 = (f32[768]{0:T(1024)}, f32[768]{0:T(1024)}, f32[394,768]{1,0:T(8,128)S(1)}, f32[768]{0:T(1024)}, bf16[394,768]{1,0:T(8,128)(2,1)}) fusion(f32[394,768]{1,0:T(8,128)} %get-tuple-element.157, f32[768]{0:T(1024)S(1)} %copy-done.29, f32[394,768]{1,0:T(8,128)} %reshape.269, f32[394]{0:T(512)} %broadcast_multiply_fusion.3, ...), kind=kOutput, calls=%fused_computation.68 | convolution fusion | flops 1870621440 | bytes 16244896 | tf_op jit(solution)/shard_map/dot_general | solution.py:356
  286.7 3.9 multiply_reduce_fusion
  290.8 2.7 fusion.29
  299.9 3.8 reshape.282
  303.8 22.0 %fusion.1 = f32[732,12]{0,1:T(8,128)S(1)} fusion(s32[38809]{0:T(1024)S(1)} %copy-done.25, f32[12,38809]{1,0:T(8,128)} %reshape.282), kind=kOutput, calls=%fused_computation.2 | convolution fusion | flops 712067520 | bytes 2053204 | tf_op jit(solution)/shard_map/dot_general | solution.py:356
  325.8 21.6 %fusion.38 = f32[732,12]{0,1:T(8,128)} fusion(f32[732,12]{0,1:T(8,128)S(1)} %fusion.1, s32[38809]{0:T(1024)S(1)} %copy-done.25, f32[12,38809]{1,0:T(8,128)S(1)} %copy-done.13), kind=kOutput, calls=%fused_computation.85 | convolution fusion | flops 710679168 | bytes 2088340 | tf_op jit(solution)/shard_map/dot_general | solution.py:356
  348.0 3.9 copy.200
  351.9 5.6 reshape.271
  359.9 2.4 reshape.272
  363.3 5.8 multiply_reduce_fusion.4
  369.1 7.1 %convolution_convert_fusion = bf16[768,3072]{1,0:T(8,128)(2,1)} fusion(bf16[394,3072]{1,0:T(8,128)(2,1)} %copy-done.44, f32[394,768]{1,0:T(8,128)} %copy-done.6, f32[768]{0:T(1024)S(1)} %copy-done.42, f32[768]{0:T(1024)S(1)} %copy-done.41, f32[394]{0:T(512)S(1)} %copy-done.38, f32[394]{0:T(512)S(1)} %broadcast_multiply_fusion.5), kind=kOutput, calls=%fused_computation.14 | convolution fusion | flops 1862997504 | bytes 8358992 | tf_op jit(solution)/shard_map/dot_general | solution.py:350
  377.1 5.2 convolution_convert_fusion.1
  384.2 11.7 %stack.27 = bf16[1,768,2,2,2,384]{5,4,3,2,1,0:T(2,128)(2,1)} reshape(bf16[768,3072]{1,0:T(8,128)(2,1)} %convolution_convert_fusion) | data formatting | bytes 9437184 | tf_op jit(solution)/shard_map/stack | solution.py:680
  395.9 5.3 copy.206
  401.2 2.6 dot_general.92
  403.9 6.1 %convert_bitcast_fusion = bf16[1,768,2,2,2,384]{5,1,4,3,2,0:T(8,128)(2,1)} fusion(bf16[2,2,2,384,394]{3,2,1,0,4:T(2,128)(2,1)} %dot_general.92, bf16[394,768,1,1,1]{1,0,2,3,4:T(8,128)(2,1)S(1)} %copy-done.20), kind=kOutput, calls=%fused_computation.36 | convolution fusion | flops 1861484544 | bytes 7744512 | tf_op jit(solution)/shard_map/dot_general | solution.py:350
  410.0 8.5 %maximum_bitcast_fusion = bf16[2,2,2,2,768,384]{5,4,1,3,2,0:T(8,128)(2,1)} fusion(bf16[1,768,2,2,2,384]{5,1,4,3,2,0:T(8,128)(2,1)} %convert_bitcast_fusion, bf16[1,768,2,2,2,384]{5,1,4,3,2,0:T(8,128)(2,1)} %copy.206), kind=kLoop, calls=%fused_computation.12 | loop fusion | flops 4718592 | bytes 18874368 | tf_op jit(solution)/shard_map/transpose | solution.py:681
  418.5 8.5 %copy.207 = bf16[2,2,2,2,768,384]{5,4,3,2,1,0:T(8,128)(2,1)} copy(bf16[2,2,2,2,768,384]{5,4,1,3,2,0:T(8,128)(2,1)} %maximum_bitcast_fusion) | data formatting | bytes 18874368 | tf_op jit(solution)/shard_map/transpose | solution.py:681
  427.0 4.5 copy.202
  431.5 5.4 copy.203
  437.0 8.7 %concatenate.22 = bf16[3,2,4,2,2,48,384]{6,5,4,3,2,1,0:T(8,128)(2,1)S(1)} reshape(bf16[3,2,768,3,128]{4,3,2,1,0:T(4,128)(2,1)} %copy.203) | data formatting | bytes 7077888 | tf_op jit(solution)/shard_map/concatenate | solution.py:674
  448.0 4.0 pad_maximum_fusion.narrow_in
  452.1 91.9 %shard_map.332 = (f32[4,2,24,384]{3,2,1,0:T(8,128)}, f32[4,96,384]{2,1,0:T(8,128)}) custom-call(bf16[4,2,4,2,2,48,384]{6,5,4,3,2,1,0:T(8,128)(2,1)} %pad_maximum_fusion.narrow_in, bf16[4,2,2,4,2,96,384]{6,5,4,3,2,1,0:T(8,128)(2,1)} %bitcast.141), custom_call_target="tpu_custom_call" | custom-call | tf_op jit(solution)/shard_map/pallas_call | solution.py:281
  (178 shorter events, 77.3 us)
Async XLA Ops:
  7.2 549.2 %all-reduce.3.cloned.1.call-start = ((), (), s32[]{:S(2)}) async-start(), calls=%async_computation | async-start | bytes 204800 | tf_op jit(solution)/shard_map/psum | solution.py:691
  98.2 2.5 copy-start.3
  108.2 10.0 %copy-start.26 = (f32[768]{0:T(1024)S(1)}, f32[768]{0:T(1024)}, u32[]{:S(2)}) copy-start(f32[768]{0:T(1024)} %param.24) | copy-start | bytes 9220
  108.2 10.0 %copy-start.31 = (f32[768]{0:T(1024)S(1)}, f32[768]{0:T(1024)}, u32[]{:S(2)}) copy-start(f32[768]{0:T(1024)} %param.25) | copy-start | bytes 9220
  114.7 9.6 %copy-start = (bf16[768,3,2,3,128]{0,4,3,2,1:T(8,128)(2,1)}, bf16[768,3,2,3,128]{0,4,3,2,1:T(8,128)(2,1)S(1)}, u32[]{:S(2)}) copy-start(bf16[768,3,2,3,128]{0,4,3,2,1:T(8,128)(2,1)S(1)} %copy.183) | copy-start | bytes 10616836
  118.2 3.1 copy-start.15
  118.3 6.0 %copy-start.34 = (f32[768]{0:T(1024)S(1)}, f32[768]{0:T(1024)}, u32[]{:S(2)}) copy-start(f32[768]{0:T(1024)} %param.28) | copy-start | bytes 9220
  118.3 6.0 %copy-start.35 = (f32[768]{0:T(1024)S(1)}, f32[768]{0:T(1024)}, u32[]{:S(2)}) copy-start(f32[768]{0:T(1024)} %param.27) | copy-start | bytes 9220
  140.7 3.2 copy-start.23
  140.7 3.5 copy-start.39
  144.2 19.7 %copy-start.24 = (s32[38809]{0:T(1024)}, s32[38809]{0:T(1024)S(1)}, u32[]{:S(2)}) copy-start(s32[38809]{0:T(1024)S(1)} %eq.44) | copy-start | bytes 465712
  186.7 3.6 copy-start.36
  186.7 3.6 copy-start.22
  198.0 2.3 copy-start.5
  202.4 4.1 copy-start.29
  202.4 4.1 copy-start.32
  209.9 1.1 copy-start.6
  227.2 8.9 %copy-start.33 = (f32[768]{0:T(1024)S(1)}, f32[768]{0:T(1024)}, u32[]{:S(2)}) copy-start(f32[768]{0:T(1024)} %param.38) | copy-start | bytes 9220
  241.6 5.9 %copy-start.21 = (bf16[394,768]{1,0:T(8,128)(2,1)S(1)}, bf16[394,768]{1,0:T(8,128)(2,1)}, u32[]{:S(2)}) copy-start(bf16[394,768]{1,0:T(8,128)(2,1)} %convert_element_type.116) | copy-start | bytes 1815556
  241.6 24.1 %slice-start.2 = ((s8[4718592]{0:T(1024)(128)(4,1)}), s8[524288]{0:T(1024)(128)(4,1)S(1)}, s32[]{:S(2)}) async-start(s8[4718592]{0:T(1024)(128)(4,1)} %bitcast.161), calls=%async_computation.3 | async-start | bytes 1048576
  247.5 18.2 %copy-start.43 = (f32[394,3072]{1,0:T(8,128)}, f32[394,3072]{1,0:T(8,128)S(1)}, u32[]{:S(2)}) copy-start(f32[394,3072]{1,0:T(8,128)S(1)} %get-tuple-element.163) | copy-start | bytes 14524420
  247.5 18.2 %copy-start.7 = (f32[394,768]{1,0:T(8,128)S(1)}, f32[394,768]{1,0:T(8,128)}, u32[]{:S(2)}) copy-start(f32[394,768]{1,0:T(8,128)} %copy-done.6) | copy-start | bytes 3631108
  247.5 18.2 %slice-start.3 = ((s8[4718592]{0:T(1024)(128)(4,1)}), s8[4194304]{0:T(1024)(128)(4,1)S(1)}, s32[]{:S(2)}) async-start(s8[4718592]{0:T(1024)(128)(4,1)} %bitcast.161), calls=%async_computation.4 | async-start | bytes 8388608
  247.5 18.2 %copy-start.37 = (f32[394]{0:T(512)S(1)}, f32[394]{0:T(512)}, u32[]{:S(2)}) copy-start(f32[394]{0:T(512)} %add_rsqrt_fusion.1) | copy-start | bytes 4732
  247.5 18.2 %copy-start.40 = (f32[768]{0:T(1024)S(1)}, f32[768]{0:T(1024)}, u32[]{:S(2)}) copy-start(f32[768]{0:T(1024)} %param.32) | copy-start | bytes 9220
  265.7 3.9 copy-start.44
  284.0 2.7 copy-start.28
  286.7 3.9 slice-start
  286.7 4.0 slice-start.1
  294.1 1.8 copy-start.18
  295.9 1.8 copy-start.2
  299.9 3.8 copy-start.25
  303.8 22.0 %copy-start.13 = (f32[12,38809]{1,0:T(8,128)S(1)}, f32[12,38809]{1,0:T(8,128)}, u32[]{:S(2)}) copy-start(f32[12,38809]{1,0:T(8,128)} %reshape.282) | copy-start | bytes 5588500
  325.8 21.7 %copy-start.12 = (bf16[1,2,12,197,64]{3,4,2,1,0:T(8,128)(2,1)S(1)}, bf16[1,2,12,197,64]{3,4,2,1,0:T(8,128)(2,1)}, u32[]{:S(2)}) copy-start(bf16[1,2,12,197,64]{3,4,2,1,0:T(8,128)(2,1)} %fusion.35) | copy-start | bytes 1815556
  325.8 21.7 %copy-start.17 = (bf16[1,2,12,197,64]{3,4,2,1,0:T(8,128)(2,1)S(1)}, bf16[1,2,12,197,64]{3,4,2,1,0:T(8,128)(2,1)}, u32[]{:S(2)}) copy-start(bf16[1,2,12,197,64]{3,4,2,1,0:T(8,128)(2,1)} %fusion.33) | copy-start | bytes 1815556
  363.3 5.8 %copy-start.38 = (f32[394]{0:T(512)S(1)}, f32[394]{0:T(512)}, u32[]{:S(2)}) copy-start(f32[394]{0:T(512)} %add_rsqrt_fusion.1) | copy-start | bytes 4732
  363.3 5.8 %copy-start.41 = (f32[768]{0:T(1024)S(1)}, f32[768]{0:T(1024)}, u32[]{:S(2)}) copy-start(f32[768]{0:T(1024)} %param.32) | copy-start | bytes 9220
  363.3 5.8 %copy-start.42 = (f32[768]{0:T(1024)S(1)}, f32[768]{0:T(1024)}, u32[]{:S(2)}) copy-start(f32[768]{0:T(1024)} %param.33) | copy-start | bytes 9220
  369.1 7.1 %copy-start.4 = (bf16[2,197,768]{2,1,0:T(8,128)(2,1)S(1)}, bf16[2,197,768]{2,1,0:T(8,128)(2,1)}, u32[]{:S(2)}) copy-start(bf16[2,197,768]{2,1,0:T(8,128)(2,1)} %copy.193) | copy-start | bytes 1815556
  377.1 5.2 copy-start.9
  377.1 5.2 copy-start.11
  382.3 1.9 copy-start.16
  395.9 5.3 copy-start.14
  401.2 2.7 copy-start.20
  452.1 93.7 %copy-start.30 = (f32[394]{0:T(512)S(1)}, f32[394]{0:T(512)}, u32[]{:S(2)}) copy-start(f32[394]{0:T(512)} %get-tuple-element.119) | copy-start | bytes 4732
  452.1 93.8 %copy-start.1 = (f32[394,768]{1,0:T(8,128)S(1)}, f32[394,768]{1,0:T(8,128)}, u32[]{:S(2)}) copy-start(f32[394,768]{1,0:T(8,128)} %reshape.272) | copy-start | bytes 3631108
  452.1 93.8 %copy-start.10 = (f32[394,768]{1,0:T(8,128)S(1)}, f32[394,768]{1,0:T(8,128)}, u32[]{:S(2)}) copy-start(f32[394,768]{1,0:T(8,128)} %copy-done.8) | copy-start | bytes 3631108
  549.5 5.5 copy-start.19
  (2 other events, 1.7 us)
Sparse Core Ops, SparseCore 0:
  369.2 130.4 all-reduce.2

commit v2 on v0

--- a/solution.py
+++ b/solution.py
@@ -1,11 +1,787 @@
 import jax
 import jax.numpy as jnp
 from jax import lax
+from jax.experimental import pallas as pl
+from jax.experimental.pallas import tpu as pltpu
 from jax.sharding import PartitionSpec as P
 
 EPS = 1e-06
 ROOT_HALF = 0.7071067811865476
 DENSITY = 0.3989422804014327
+
+
+MESH = pl.DeviceIdType.MESH
+KINDS = (0, 0, 0, 0, 1, 1, 1, 1)
+SLOT = (0, 1, 2, 3, 0, 1, 2, 3)
+GATHER_Y_LAST = (True, False, True, False, True, False, True, False)
+REDUCE_X_LAST = (True, False, True, False, True, True, False, False)
+N_COPY = 10
+PAD = 208
+TALL = 2 * PAD
+KEYS = 256
+TILE = 384
+
+
+def place():
+    dp = lax.axis_index("dp")
+    mlp = lax.axis_index("mlp")
+    return lax.div(dp, 2), lax.rem(dp, 2), lax.div(mlp, 2), lax.rem(mlp, 2)
+
+
+def device(z, x, y, c):
+    return (z * 2 + x, y * 2 + c)
+
+
+def own(ref, kind, z, x, y, c):
+    return ref.at[c, z, x, y] if kind == 0 else ref.at[y, c, z, x]
+
+
+def line(ref, kind, x, y, c):
+    return ref.at[c, :, x, y] if kind == 0 else ref.at[y, c, :, x]
+
+
+def greet(z, x, y, c):
+    barrier = pltpu.get_barrier_semaphore()
+    others = [device(lax.rem(z + d, 4), x, y, c) for d in (1, 2, 3)]
+    others += [device(z, 1 - x, y, c), device(z, x, 1 - y, c), device(z, 1 - x, 1 - y, c), device(z, x, y, 1 - c)]
+    for other in others:
+        pl.semaphore_signal(barrier, inc=1, device_id=other, device_id_type=MESH)
+    pl.semaphore_wait(barrier, len(others))
+
+
+class Link:
+    def __init__(self, send, recv):
+        self.send, self.recv, self.pending = send, recv, []
+
+    def copy(self, src, dst, slot, target):
+        made = pltpu.make_async_remote_copy(
+            src_ref=src,
+            dst_ref=dst,
+            send_sem=self.send.at[slot],
+            recv_sem=self.recv.at[slot],
+            device_id=target,
+            device_id_type=MESH,
+        )
+        made.start()
+        self.pending.append(made)
+        return made
+
+    def drain(self):
+        for made in self.pending:
+            made.wait_send()
+        self.pending = []
+
+
+class Gather:
+    def __init__(self, link, ref, unit, where):
+        self.link, self.ref, self.where = link, ref, where
+        self.kind = KINDS[unit]
+        self.base = unit * N_COPY
+        self.y_last = GATHER_Y_LAST[unit]
+
+    def put(self, part, slot, target):
+        return self.link.copy(part, part, self.base + slot, target)
+
+    def along_z(self):
+        z, x, y, c = self.where
+        part = own(self.ref, self.kind, z, x, y, c)
+        self.z = [self.put(part, d - 1, device(lax.rem(z + d, 4), x, y, c)) for d in (1, 2, 3)]
+
+    def line_out(self):
+        z, x, y, c = self.where
+        for made in self.z:
+            made.wait_recv()
+        part = line(self.ref, self.kind, x, y, c)
+        self.to_x = self.put(part, 3, device(z, 1 - x, y, c))
+        self.to_y = self.put(part, 4, device(z, x, 1 - y, c))
+        self.to_c = [self.put(part, 6, device(z, x, y, 1 - c))]
+
+    def plane_out(self):
+        z, x, y, c = self.where
+        mirror = device(z, x, y, 1 - c)
+        from_x = line(self.ref, self.kind, 1 - x, y, c)
+        from_y = line(self.ref, self.kind, x, 1 - y, c)
+        if self.y_last:
+            self.to_x.wait_recv()
+            self.last = self.put(from_x, 5, device(z, x, 1 - y, c))
+            self.to_c.append(self.put(from_x, 7, mirror))
+            self.to_y.wait_recv()
+            self.to_c.append(self.put(from_y, 8, mirror))
+        else:
+            self.to_y.wait_recv()
+            self.last = self.put(from_y, 5, device(z, 1 - x, y, c))
+            self.to_c.append(self.put(from_y, 7, mirror))
+            self.to_x.wait_recv()
+            self.to_c.append(self.put(from_x, 8, mirror))
+
+    def core_out(self):
+        z, x, y, c = self.where
+        self.last.wait_recv()
+        part = line(self.ref, self.kind, 1 - x, 1 - y, c)
+        self.to_c.append(self.put(part, 9, device(z, x, y, 1 - c)))
+
+    def finish(self):
+        for made in self.to_c:
+            made.wait_recv()
+
+
+class Scatter:
+    def __init__(self, link, ref, buffers, unit, where):
+        self.link, self.ref, self.where = link, ref, where
+        self.half, self.quarter, self.eighth, self.parts = buffers
+        self.kind = KINDS[unit]
+        self.base = (8 + unit) * N_COPY
+        self.x_last = REDUCE_X_LAST[unit]
+
+    def put(self, src, dst, slot, target):
+        return self.link.copy(src, dst, self.base + slot, target)
+
+    def by_core(self, ref, c):
+        return ref.at[c] if self.kind == 0 else ref.at[:, c]
+
+    def by_y(self, ref, y, c):
+        return ref.at[c, :, :, y] if self.kind == 0 else ref.at[y, c]
+
+    def by_x(self, ref, x, c):
+        return ref.at[c, :, x] if self.kind == 0 else ref.at[:, c, :, x]
+
+    def mix(self, here, there):
+        total = here[...].astype(jnp.float32) + there[...].astype(jnp.float32)
+        here[...] = total.astype(jnp.bfloat16)
+
+    def to_core(self):
+        z, x, y, c = self.where
+        self.made = self.put(self.by_core(self.ref, 1 - c), self.half, 0, device(z, x, y, 1 - c))
+
+    def to_first(self):
+        z, x, y, c = self.where
+        self.made.wait_recv()
+        self.mix(self.by_core(self.ref, c), self.half)
+        if self.x_last:
+            self.made = self.put(self.by_y(self.ref, 1 - y, c), self.quarter, 1, device(z, x, 1 - y, c))
+        else:
+            self.made = self.put(self.by_x(self.ref, 1 - x, c), self.quarter, 1, device(z, 1 - x, y, c))
+
+    def to_second(self):
+        z, x, y, c = self.where
+        self.made.wait_recv()
+        self.mix(self.by_y(self.ref, y, c) if self.x_last else self.by_x(self.ref, x, c), self.quarter)
+        if self.x_last:
+            self.made = self.put(line(self.ref, self.kind, 1 - x, y, c), self.eighth, 2, device(z, 1 - x, y, c))
+        else:
+            self.made = self.put(line(self.ref, self.kind, x, 1 - y, c), self.eighth, 2, device(z, x, 1 - y, c))
+
+    def to_z(self):
+        z, x, y, c = self.where
+        self.made.wait_recv()
+        self.mix(line(self.ref, self.kind, x, y, c), self.eighth)
+        self.z = []
+        for d in (1, 2, 3):
+            far = lax.rem(z + d, 4)
+            src = own(self.ref, self.kind, far, x, y, c)
+            self.z.append(self.put(src, self.parts.at[d - 1], 2 + d, device(far, x, y, c)))
+
+    def total(self):
+        for made in self.z:
+            made.wait_recv()
+        total = own(self.ref, self.kind, *self.where)[...].astype(jnp.float32)
+        for d in range(3):
+            total = total + self.parts[d].astype(jnp.float32)
+        return total
+
+
+class Everywhere:
+    def __init__(self, link, ref, core_ref, plane_ref, line_ref, base, where):
+        self.link, self.ref, self.where, self.base = link, ref, where, base
+        self.core_ref, self.plane_ref, self.line_ref = core_ref, plane_ref, line_ref
+
+    def to_core(self):
+        z, x, y, c = self.where
+        self.made = [self.link.copy(self.ref, self.core_ref, self.base, device(z, x, y, 1 - c))]
+
+    def wait(self):
+        for made in self.made:
+            made.wait_recv()
+
+    def to_plane(self):
+        z, x, y, c = self.where
+        self.wait()
+        chip = self.plane_ref.at[3]
+        chip[...] = self.ref[...] + self.core_ref[...]
+        targets = (device(z, 1 - x, y, c), device(z, x, 1 - y, c), device(z, 1 - x, 1 - y, c))
+        self.made = [
+            self.link.copy(chip, self.plane_ref.at[n], self.base + 1 + n, target) for n, target in enumerate(targets)
+        ]
+
+    def to_line(self):
+        z, x, y, c = self.where
+        self.wait()
+        got = self.plane_ref
+        self.line_ref[z] = (got[3] + got[0]) + (got[1] + got[2])
+        part = self.line_ref.at[z]
+        self.made = [
+            self.link.copy(part, part, self.base + 3 + d, device(lax.rem(z + d, 4), x, y, c)) for d in (1, 2, 3)
+        ]
+
+    def total(self):
+        self.wait()
+        got = self.line_ref
+        return (got[0] + got[1]) + (got[2] + got[3])
+
+
+F32 = jnp.float32
+BF16 = jnp.bfloat16
+
+
+def dot(left, right):
+    return lax.dot_general(left, right, (((1,), (0,)), ((), ())), preferred_element_type=F32)
+
+
+def dot_nt(left, right):
+    return lax.dot_general(left, right, (((1,), (1,)), ((), ())), preferred_element_type=F32)
+
+
+def dot_tn(left, right):
+    return lax.dot_general(left, right, (((0,), (0,)), ((), ())), preferred_element_type=F32)
+
+
+def fold(values):
+    rows, width = values.shape
+    return jnp.sum(values.reshape(rows // 8, 8, width), 0)
+
+
+def unit_of(values):
+    mean = jnp.mean(values, -1, keepdims=True)
+    centred = values - mean
+    variance = jnp.mean(centred * centred, -1, keepdims=True)
+    scaled = lax.rsqrt(variance + EPS)
+    return centred * scaled, scaled
+
+
+def by_rows(step, init):
+    size = 32
+
+    def one(index, carried):
+        return step(pl.ds(pl.multiple_of(index * size, size), size), carried)
+
+    return lax.fori_loop(0, TALL // size, one, init)
+
+
+def layer_kernel(*refs):
+    (
+        tokens, cotangent, keep, places, first_gain, first_shift, query_bias, value_bias, outer_bias, attend_scale,
+        second_gain, second_shift, up_bias, down_bias, feed_scale, table, small_in, large_in,
+        result, token_grad, small_out, large_out, early_out, late_out, table_out,
+        narrow, wide, half0, half1, quarter0, quarter1a, quarter1b, eighth0, eighth1, parts0, parts1, pair, mine,
+        source, upstream, normed1, normed1_t, normed2, normed2_t, qkv, bias, mask, index, probs, mix_t, attend, resid,
+        dfeed, dfeed_t, hidden, slope, total, dnormed2, shifts, ups,
+        early, late, hits, early_core, early_plane, early_line, late_core, late_plane, late_line, hits_core, hits_plane, hits_line,
+        send, recv,
+    ) = refs
+    dresid, dproj, mix, dmixed, dattend = resid, hidden, normed2, normed2, dfeed
+    where = z, x, y, c = place()
+    greet(*where)
+    link = Link(send, recv)
+    pair[:, c] = small_in[:, c]
+    mate = link.copy(small_in.at[:, 1 - c], pair.at[:, c], 16 * N_COPY, device(z, x, y, 1 - c))
+    for unit in range(4):
+        wide[unit, y, c, z, x] = large_in[unit]
+    mate.wait_recv()
+    for unit in range(4):
+        narrow[unit, c, z, x, y] = pair[unit].reshape(48, TILE).astype(BF16)
+    gathers = [Gather(link, (narrow if KINDS[u] == 0 else wide).at[SLOT[u]], u, where) for u in range(8)]
+    for unit in gathers:
+        unit.along_z()
+
+    def advance(step):
+        if step < 8:
+            gathers[step].line_out()
+        if 0 <= step - 1 < 8:
+            gathers[step - 1].plane_out()
+        if 0 <= step - 2 < 8:
+            gathers[step - 2].core_out()
+
+    for image in range(2):
+        last = pl.ds(image * PAD + 192, 16)
+        source[last, :] = jnp.zeros((16, 768), BF16)
+        upstream[last, :] = jnp.zeros((16, 768), BF16)
+        source[pl.ds(image * PAD, 197), :] = tokens[image]
+        upstream[pl.ds(image * PAD, 197), :] = cotangent[image]
+
+    def norm_first(rows, carried):
+        unit, _ = unit_of(source[rows, :].astype(F32))
+        normed1[rows, :] = (unit * first_gain[...] + first_shift[...]).astype(BF16)
+        lifted = upstream[rows, :].astype(F32) * feed_scale[...]
+        dfeed[rows, :] = lifted.astype(BF16)
+        return carried + fold(lifted)
+
+    sum_down = by_rows(norm_first, jnp.zeros((8, 768), F32))
+    early[...] = jnp.zeros((16, 768), F32)
+    late[...] = jnp.zeros((8, 768), F32)
+    early[4:5, :] = jnp.sum(sum_down, 0, keepdims=True)
+    index[...] = jnp.full((PAD, KEYS), -1, jnp.int32)
+    index[0:197, 0:197] = places[...]
+    row_of = lax.broadcasted_iota(jnp.int32, (PAD, KEYS), 0)
+    col_of = lax.broadcasted_iota(jnp.int32, (PAD, KEYS), 1)
+    for image in range(2):
+        mask[image] = jnp.full((PAD, KEYS), -1e30, F32)
+        kept = jnp.where(keep[image : image + 1, :] == 1, 0.0, -1e30).astype(F32)
+        mask[image, :, 0:197] = jnp.broadcast_to(kept, (PAD, 197))
+        mask[image] = jnp.where(row_of == col_of, 0.0, mask[image])
+    advance(0)
+
+    def look_up(head, carried):
+        for side in range(2):
+            cols = slice(side * 128, side * 128 + 128)
+            spot = index[:, cols]
+            low, high = spot & 127, spot >> 7
+            found = jnp.zeros((PAD, 128), F32)
+            for piece in range(6):
+                row = table[head, :, piece * 128 : piece * 128 + 128]
+                picked = jnp.take_along_axis(jnp.broadcast_to(row, (PAD, 128)), low, axis=1)
+                found = jnp.where(high == piece, picked, found)
+            bias[head, :, cols] = found
+        return carried
+
+    advance(1)
+    lax.fori_loop(0, 12, look_up, 0)
+    advance(2)
+    zero_row = jnp.zeros((1, 128), F32)
+    for p in range(6):
+        cols = slice(p * 128, p * 128 + 128)
+        shifts[p] = jnp.concatenate([query_bias[:, cols], zero_row, value_bias[:, cols]], axis=1)
+        qkv[p, TALL:, :] = jnp.zeros((48, TILE), BF16)
+    normed1_t[...] = normed1[...].T
+    dfeed_t[...] = dfeed[...].T
+    lane = lax.broadcasted_iota(jnp.int32, (1, 128), 1)
+    picks = [(lane < 64).astype(F32).astype(BF16), (lane >= 64).astype(F32).astype(BF16)]
+    first_half = lax.broadcasted_iota(jnp.int32, (PAD, 128), 1) < 64
+    scaling = jnp.where(lax.broadcasted_iota(jnp.int32, (1, TILE), 1) < 128, 0.125, 1.0).astype(F32)
+    advance(3)
+
+    def rows_of(image):
+        return pl.ds(pl.multiple_of(image * PAD, 16), PAD)
+
+    def keys_of(image):
+        return pl.ds(pl.multiple_of(image * PAD, 16), KEYS)
+
+    def cols_of(p):
+        return pl.ds(pl.multiple_of(p * 128, 128), 128)
+
+    for k in range(3):
+        gathers[k].finish()
+
+        def project(core, carried, k=k):
+            p = core * 3 + k
+            weight = narrow[k, core].reshape(768, TILE)
+            value = (dot(normed1[...], weight) + shifts[p]).astype(BF16)
+            qkv[p, 0:TALL, :] = (value.astype(F32) * scaling).astype(BF16)
+            return carried
+
+        lax.fori_loop(0, 2, project, 0)
+
+        def attend_pair(step, carried, k=k):
+            core, image = step // 2, step % 2
+            p = core * 3 + k
+            query = qkv[p, rows_of(image), 0:128]
+            keys = qkv[p, keys_of(image), 128:256]
+            values = qkv[p, keys_of(image), 256:384]
+            outs = []
+            for t in range(2):
+                logits = dot_nt(query * picks[t], keys) + bias[2 * p + t] + mask[image]
+                top = jnp.max(logits, -1, keepdims=True)
+                expd = jnp.exp(logits - top)
+                share = (expd * (1.0 / jnp.sum(expd, -1, keepdims=True))).astype(BF16)
+                probs[image, 2 * p + t] = share
+                outs.append(dot(share, values))
+            mix[rows_of(image), cols_of(p)] = jnp.where(first_half, outs[0], outs[1]).astype(BF16)
+            return carried
+
+        lax.fori_loop(0, 4, attend_pair, 0)
+        advance(4 + k)
+    gathers[3].finish()
+    for core in range(2):
+        cols = slice(core * TILE, core * TILE + TILE)
+        attend[:, cols] = dot(mix[...], narrow[3, core].reshape(768, TILE)) + outer_bias[:, cols]
+    mix_t[...] = mix[...].T
+    advance(7)
+
+    def norm_second(rows, carried):
+        value = source[rows, :].astype(F32) + attend_scale[...] * attend[rows, :]
+        resid[rows, :] = value
+        unit, _ = unit_of(value)
+        normed2[rows, :] = (unit * second_gain[...] + second_shift[...]).astype(BF16)
+        total[rows, :] = jnp.zeros((32, 768), F32)
+        dnormed2[rows, :] = jnp.zeros((32, 768), F32)
+        return carried
+
+    by_rows(norm_second, 0)
+    normed2_t[...] = normed2[...].T
+
+    def up_cols(k, block):
+        return pl.ds(pl.multiple_of(block * 768 + k * TILE, 128), TILE)
+
+    for k in range(2):
+        gathers[4 + k].finish()
+
+        def widen(block, carried, k=k):
+            weight = wide[k, block // 2, block % 2].reshape(768, TILE)
+            pre = dot(normed2[...], weight) + up_bias[:, up_cols(k, block)]
+            cumul = 0.5 * (1.0 + lax.erf(pre * ROOT_HALF))
+            hidden[k * 4 + block] = (pre * cumul).astype(BF16)
+            slope[k * 4 + block] = (cumul + pre * jnp.exp(-0.5 * pre * pre) * DENSITY).astype(BF16)
+            return carried
+
+        lax.fori_loop(0, 4, widen, 0)
+        advance(8 + k)
+    gathers[6].finish()
+    gathers[7].finish()
+    link.drain()
+    scatters = []
+    for u in range(8):
+        s = SLOT[u]
+        if KINDS[u] == 0:
+            buffers = (half0.at[s], quarter0.at[s], eighth0.at[s], parts0.at[s])
+        else:
+            quarter1 = quarter1a if REDUCE_X_LAST[u] else quarter1b
+            buffers = (half1.at[s], quarter1.at[s % 2], eighth1.at[s], parts1.at[s])
+        scatters.append(Scatter(link, (narrow if KINDS[u] == 0 else wide).at[s], buffers, u, where))
+
+    for k in range(2):
+
+        def narrow_back(block, carried, k=k):
+            b = k * 4 + block
+            down = wide[2 + k, block // 2, block % 2].reshape(768, TILE)
+            total[...] += dot_nt(hidden[b], down)
+            dpre = (dot(dfeed[...], down) * slope[b].astype(F32)).astype(BF16)
+            ups[b] = jnp.sum(fold(dpre.astype(F32)), 0, keepdims=True)
+            up = wide[k, block // 2, block % 2].reshape(768, TILE)
+            dnormed2[...] += dot_nt(dpre, up)
+            shape = (4, 2, 96, TILE)
+            wide[2 + k, block // 2, block % 2] = dot(normed2_t[...], dpre).astype(BF16).reshape(shape)
+            wide[k, block // 2, block % 2] = dot(dfeed_t[...], hidden[b]).astype(BF16).reshape(shape)
+            return carried
+
+        lax.fori_loop(0, 4, narrow_back, 0)
+        scatters[4 + k].to_core()
+        scatters[6 + k].to_core()
+    scatters[4].to_first()
+    scatters[6].to_first()
+
+    def second_back(rows, carried):
+        feed_scale_sum, gain_sum, shift_sum, scale_sum, bias_sum = carried
+        feed = total[rows, :] + down_bias[...]
+        above = upstream[rows, :].astype(F32)
+        value = resid[rows, :]
+        total[rows, :] = value + feed_scale[...] * feed
+        unit, scaled = unit_of(value)
+        grad = dnormed2[rows, :]
+        inner = grad * second_gain[...]
+        first = jnp.mean(inner, -1, keepdims=True)
+        second = jnp.mean(inner * unit, -1, keepdims=True)
+        back = above + scaled * (inner - first - unit * second)
+        dresid[rows, :] = back
+        lifted = attend_scale[...] * back
+        dattend[rows, :] = lifted.astype(BF16)
+        return (
+            feed_scale_sum + fold(feed * above),
+            gain_sum + fold(grad * unit),
+            shift_sum + fold(grad),
+            scale_sum + fold(attend[rows, :] * back),
+            bias_sum + fold(lifted),
+        )
+
+    zero = jnp.zeros((8, 768), F32)
+    sums = by_rows(second_back, (zero,) * 5)
+    for b in range(8):
+        early[8 + b : 9 + b, 0:TILE] = ups[b]
+    for row, value in zip((5, 2, 3, 1, 0), sums):
+        early[row : row + 1, :] = jnp.sum(value, 0, keepdims=True)
+    for image in range(2):
+        result[image] = total[pl.ds(image * PAD, 197), :].astype(BF16)
+    everywhere = Everywhere(link, early, early_core, early_plane, early_line, 16 * N_COPY + 5, where)
+    everywhere.to_core()
+    scatters[5].to_first()
+    scatters[7].to_first()
+    half_mixed = [
+        dot_nt(dattend[:, core * TILE : core * TILE + TILE], narrow[3, core].reshape(768, TILE)) for core in range(2)
+    ]
+    dmixed[...] = (half_mixed[0] + half_mixed[1]).astype(BF16)
+    for core in range(2):
+        cols = slice(core * TILE, core * TILE + TILE)
+        narrow[3, core] = dot(mix_t[...], dattend[:, cols]).astype(BF16).reshape(4, 2, 2, 48, TILE)
+    scatters[3].to_core()
+    everywhere.to_plane()
+    total[...] = jnp.zeros((TALL, 768), F32)
+
+    def service(k):
+        if k == 0:
+            scatters[3].to_first()
+            scatters[4].to_second()
+            scatters[6].to_second()
+        if k == 1:
+            scatters[0].to_first()
+            scatters[5].to_second()
+            scatters[7].to_second()
+            scatters[4].to_z()
+            scatters[6].to_z()
+            everywhere.to_line()
+        if k == 2:
+            scatters[1].to_first()
+            scatters[3].to_second()
+            scatters[0].to_second()
+            scatters[5].to_z()
+            scatters[7].to_z()
+
+    for k in range(3):
+
+        def attend_back(step, carried, k=k):
+            core, image = step // 2, step % 2
+            p = core * 3 + k
+            query = qkv[p, rows_of(image), 0:128]
+            keys = qkv[p, keys_of(image), 128:256]
+            values = qkv[p, keys_of(image), 256:384]
+            above = dmixed[rows_of(image), cols_of(p)]
+            dquery, dkeys, dvalues = [], [], []
+            for t in range(2):
+                share = probs[image, 2 * p + t]
+                dvalues.append(dot_tn(share, above)[0:PAD])
+                dshare = dot_nt(above * picks[t], values)
+                full = share.astype(F32)
+                dlogits = full * (dshare - jnp.sum(dshare * full, -1, keepdims=True))
+                bias[2 * p + t] = jnp.where(image == 0, 0.0, bias[2 * p + t]) + dlogits
+                low = dlogits.astype(BF16)
+                dquery.append(dot(low, keys) * 0.125)
+                dkeys.append(dot_tn(low, query)[0:PAD])
+            rows = rows_of(image)
+            dproj[p, rows, 0:128] = jnp.where(first_half, dquery[0], dquery[1]).astype(BF16)
+            dproj[p, rows, 128:256] = jnp.where(first_half, dkeys[0], dkeys[1]).astype(BF16)
+            dproj[p, rows, 256:384] = jnp.where(first_half, dvalues[0], dvalues[1]).astype(BF16)
+            return carried
+
+        lax.fori_loop(0, 4, attend_back, 0)
+
+        def project_back(core, carried, k=k):
+            p = core * 3 + k
+            grad = dproj[p]
+            summed = jnp.sum(fold(grad.astype(F32)), 0, keepdims=True)
+            late[2:3, cols_of(p)] = summed[:, 0:128]
+            late[3:4, cols_of(p)] = summed[:, 256:384]
+            total[...] += dot_nt(grad, narrow[k, core].reshape(768, TILE))
+            narrow[k, core] = dot(normed1_t[...], grad).astype(BF16).reshape(4, 2, 2, 48, TILE)
+            return carried
+
+        lax.fori_loop(0, 2, project_back, 0)
+        scatters[k].to_core()
+        service(k)
+
+    def first_back(rows, carried):
+        gain_sum, shift_sum = carried
+        grad = total[rows, :]
+        unit, scaled = unit_of(source[rows, :].astype(F32))
+        inner = grad * first_gain[...]
+        first = jnp.mean(inner, -1, keepdims=True)
+        second = jnp.mean(inner * unit, -1, keepdims=True)
+        dresid[rows, :] = dresid[rows, :] + scaled * (inner - first - unit * second)
+        return gain_sum + fold(grad * unit), shift_sum + fold(grad)
+
+    sums = by_rows(first_back, (zero, zero))
+    late[0:1, :] = jnp.sum(sums[0], 0, keepdims=True)
+    late[1:2, :] = jnp.sum(sums[1], 0, keepdims=True)
+    scatters[2].to_first()
+    late_sum = Everywhere(link, late, late_core, late_plane, late_line, 16 * N_COPY + 15, where)
+    late_sum.to_core()
+    for image in range(2):
+        token_grad[image] = dresid[pl.ds(image * PAD, 197), :].astype(BF16)
+    mates = []
+
+    def settle(u):
+        s = SLOT[u]
+        value = scatters[u].total()
+        if KINDS[u] == 0:
+            mine[s] = value.reshape(2, 24, TILE)
+            small_out[s, c] = mine[s, c]
+            mates.append(link.copy(mine.at[s, 1 - c], small_out.at[s, c], 16 * N_COPY + 1 + s, device(z, x, y, 1 - c)))
+        else:
+            large_out[s] = value
+
+    late_sum.to_plane()
+    scatters[1].to_second()
+    scatters[3].to_z()
+    scatters[0].to_z()
+    hits[...] = jnp.zeros((96, 128), F32)
+    low_of = lax.broadcasted_iota(jnp.int32, (8, KEYS), 0)
+    high_of = lax.broadcasted_iota(jnp.int32, (128, KEYS), 0)
+
+    def count(group, carried):
+        eight = pl.ds(pl.multiple_of(group * 8, 8), 8)
+        spots = index[eight, :]
+        for r in range(8):
+            spot = jnp.broadcast_to(spots[r : r + 1, :], (8, KEYS))
+            low = (spot & 7) == low_of
+            parts = []
+            for head in range(12):
+                grads = bias[head, eight, :]
+                parts.append(jnp.where(low, jnp.broadcast_to(grads[r : r + 1, :], (8, KEYS)), 0.0))
+            spread = jnp.concatenate(parts, axis=0).astype(BF16)
+            high = jnp.concatenate([spot >> 3] * 16, axis=0)
+            which = (high == high_of).astype(F32).astype(BF16)
+            carried = carried + dot_nt(spread, which)
+        return carried
+
+    hits[...] = lax.fori_loop(0, 25, count, jnp.zeros((96, 128), F32))
+    hits_sum = Everywhere(link, hits, hits_core, hits_plane, hits_line, 16 * N_COPY + 25, where)
+    hits_sum.to_core()
+    scatters[2].to_second()
+    scatters[1].to_z()
+    late_sum.to_line()
+    hits_sum.to_plane()
+    settle(4)
+    settle(6)
+    settle(5)
+    settle(7)
+    early_out[...] = everywhere.total()
+    scatters[2].to_z()
+    settle(3)
+    settle(0)
+    hits_sum.to_line()
+    settle(1)
+    settle(2)
+    late_out[...] = late_sum.total()
+    table_out[...] = hits_sum.total()
+    for made in mates:
+        made.wait_recv()
+    link.drain()
+
+
+def run_layer(*operands):
+    def vmem(*shape, dtype=BF16):
+        return pltpu.VMEM(shape, dtype)
+
+    scratch = [
+        vmem(4, 2, 4, 2, 2, 48, TILE),
+        vmem(4, 2, 2, 4, 2, 96, TILE),
+        vmem(4, 4, 2, 2, 48, TILE),
+        vmem(4, 2, 4, 2, 96, TILE),
+        vmem(4, 4, 2, 48, TILE),
+        vmem(2, 4, 2, 96, TILE),
+        vmem(2, 2, 4, 96, TILE),
+        vmem(4, 4, 48, TILE),
+        vmem(4, 4, 96, TILE),
+        vmem(4, 3, 48, TILE),
+        vmem(4, 3, 96, TILE),
+        vmem(4, 2, 24, TILE, dtype=F32),
+        vmem(4, 2, 24, TILE, dtype=F32),
+        vmem(TALL, 768),
+        vmem(TALL, 768),
+        vmem(TALL, 768),
+        vmem(768, TALL),
+        vmem(TALL, 768),
+        vmem(768, TALL),
+        vmem(6, TALL + 48, TILE),
+        vmem(12, PAD, KEYS, dtype=F32),
+        vmem(2, PAD, KEYS, dtype=F32),
+        vmem(PAD, KEYS, dtype=jnp.int32),
+        vmem(2, 12, PAD, KEYS),
+        vmem(768, TALL),
+        vmem(TALL, 768, dtype=F32),
+        vmem(TALL, 768, dtype=F32),
+        vmem(TALL, 768),
+        vmem(768, TALL),
+        vmem(8, TALL, TILE),
+        vmem(8, TALL, TILE),
+        vmem(TALL, 768, dtype=F32),
+        vmem(TALL, 768, dtype=F32),
+        vmem(6, 1, TILE, dtype=F32),
+        vmem(8, 1, TILE, dtype=F32),
+        vmem(16, 768, dtype=F32),
+        vmem(8, 768, dtype=F32),
+        vmem(96, 128, dtype=F32),
+    ]
+    for shape in ((16, 768), (8, 768), (96, 128)):
+        scratch += [vmem(*shape, dtype=F32), vmem(4, *shape, dtype=F32), vmem(4, *shape, dtype=F32)]
+    copies = 16 * N_COPY + 40
+    scratch += [pltpu.SemaphoreType.DMA((copies,)), pltpu.SemaphoreType.DMA((copies,))]
+    return pl.pallas_call(
+        layer_kernel,
+        out_shape=(
+            jax.ShapeDtypeStruct((2, 197, 768), BF16),
+            jax.ShapeDtypeStruct((2, 197, 768), BF16),
+            jax.ShapeDtypeStruct((4, 2, 24, TILE), F32),
+            jax.ShapeDtypeStruct((4, 96, TILE), F32),
+            jax.ShapeDtypeStruct((16, 768), F32),
+            jax.ShapeDtypeStruct((8, 768), F32),
+            jax.ShapeDtypeStruct((96, 128), F32),
+        ),
+        in_specs=[pl.BlockSpec(memory_space=pltpu.VMEM)] * len(operands),
+        out_specs=[pl.BlockSpec(memory_space=pltpu.VMEM)] * 7,
+        scratch_shapes=scratch,
+        compiler_params=pltpu.CompilerParams(
+            collective_id=0, has_side_effects=True, vmem_limit_bytes=62 * 2**20
+        ),
+    )(*operands)
+
+
+def fast_body(
+    tokens,
+    keep_mask,
+    position_index,
+    cotangent,
+    first_gain,
+    first_shift,
+    inner_weight,
+    query_bias,
+    value_bias,
+    outer_weight,
+    outer_bias,
+    attend_scale,
+    second_gain,
+    second_shift,
+    up_weight,
+    up_bias,
+    down_weight,
+    down_bias,
+    feed_scale,
+    position_table,
+):
+    inner_piece = inner_weight.reshape(24, 3, 2, 3, 128).transpose(3, 2, 0, 1, 4).reshape(3, 2, 24, TILE)
+    outer_piece = outer_weight.reshape(24, 2, TILE).transpose(1, 0, 2)[None]
+    small = jnp.concatenate([inner_piece, outer_piece]).astype(F32)
+    large = jnp.concatenate(
+        [up_weight.reshape(96, 2, TILE).transpose(1, 0, 2), down_weight.T.reshape(96, 2, TILE).transpose(1, 0, 2)]
+    )
+    table = jnp.pad(position_table.T, ((0, 0), (0, 36))).reshape(12, 1, 768)
+    vectors = [first_gain, first_shift, query_bias, value_bias, outer_bias, attend_scale, second_gain, second_shift]
+    vectors = [v.reshape(1, -1) for v in (*vectors, up_bias, down_bias, feed_scale)]
+    result, token_grad, small_out, large_out, early, late, hits = run_layer(
+        tokens, cotangent, keep_mask, position_index, *vectors, table, small, large
+    )
+    gradient_inner = small_out[:3].reshape(3, 2, 24, 3, 128).transpose(2, 3, 1, 0, 4).reshape(24, 2304)
+    gradient_outer = small_out[3].transpose(1, 0, 2).reshape(24, 768)
+    gradient_down = large_out[:2].transpose(1, 0, 2).reshape(96, 768).T
+    gradient_up = large_out[2:].transpose(1, 0, 2).reshape(96, 768)
+    up_bias_grad = early[8:, :TILE].reshape(2, 4, TILE).transpose(1, 0, 2).reshape(3072)
+    table_grad = hits.reshape(12, 8, 128).transpose(2, 1, 0).reshape(1024, 12)[:732]
+    return (
+        result,
+        token_grad,
+        gradient_inner,
+        gradient_outer,
+        gradient_up,
+        gradient_down,
+        late[0],
+        late[1],
+        late[2],
+        late[3],
+        early[0],
+        early[1],
+        early[2],
+        early[3],
+        up_bias_grad,
+        early[4],
+        early[5],
+        table_grad,
+    )
 
 
 def layer_norm(values, gain, shift):
@@ -276,6 +1052,7 @@
 
 
 def solution(mesh):
+    special = mesh.shape["dp"] == 8 and mesh.shape["mlp"] == 4
     placed = (
         P(None, ("dp", "mlp"), None),
         P(None, ("dp", "mlp")),
@@ -299,7 +1076,7 @@
         P(),
     )
     return jax.shard_map(
-        body,
+        fast_body if special else body,
         mesh=mesh,
         in_specs=placed,
         out_specs=(

time: 1440 us -> 226 us (0.16)
  waiting for transfers between devices: 580 us -> 0 us
  other arithmetic: 441 us -> 1.49 us
  local copies, waits for them, and re-layouts: 257 us -> 20.8 us
  Pallas kernels: 0 us -> 202 us
  matrix products: 83.5 us -> 0 us
  blocking collectives: 46.6 us -> 0 us
  between operations: 16 us -> 0.91 us
    scatter-add x2 -> x0, other arithmetic: 415 us -> none  [body(): sum_table_heads.at[:, flat_index].add(dlogits.reshape(heads, rows * rows))]
    reduce_scatter x4 -> x0, waiting for transfers between devices: 375 us -> none  [the longest x1 125 us: body(): lax.psum_scatter(sum_inner, ('dp', 'mlp'), scatter_dimension=0, tiled=True)]
    pallas_call x0 -> x1, Pallas kernels: none -> 202 us  [run_layer(): pl.pallas_call(layer_kernel, out_shape=(jax.ShapeDtypeStruct((2, 197, 768...]
    gather x4 -> x0, local copies, waits for them, and re-layouts: 145 us -> none  [body(): bias = table_by_head[:, position_index]]
    psum x1 -> x0, waiting for transfers between devices: 103 us -> none  [body(): lax.psum((sum_first_gain, sum_first_shift, sum_query_bias, sum_value_bias...]
    all_gather x8 -> x0, waiting for transfers between devices: 99.2 us -> none  [the longest x1 40.6 us: fetch(): lax.all_gather(up_weight, 'dp', axis=0, tiled=True)]
    dot_general x36 -> x0, matrix products: 83.5 us -> none  [the longest x8 24.6 us: contract_rows(): lax.dot_general(left, right, (((0,), (0,)), ((), ())), preferred_element_...]
    unnamed x238 -> x52, local copies, waits for them, and re-layouts: 60.9 us -> 7.72 us
  transfers between devices with their start and end apart: 17 -> 0, of which waited for: 9 -> 0; matrix products, arithmetic and copies ran while one was open for 18% -> 0% of each run, Pallas kernels for 0% -> 0%
where the time goes in v2:
time: 226 us; the launch traced here: 225 us
  Pallas kernels  202 us (89%)
  local copies, waits for them, and re-layouts  20.8 us (9%)
    pallas_call x1, Pallas kernels, run_layer(): pl.pallas_call(layer_kernel, out_shape=(jax.ShapeDtypeStruct((2, 197, 768...  202 us
    unnamed x52, local copies, waits for them, and re-layouts  7.72 us
    reshape x10, local copies, waits for them, and re-layouts, fast_body(): v.reshape(1, -1)  5.8 us

profile of v2, /device:TPU:0, one launch (start us, length us, event | category | flops | bytes accessed | tf_op | source)
XLA Modules:
  0.0 225.4 jit_solution(7977928402481811618)
XLA Ops:
  0.8 0.6 copy-done.13
  1.3 0.6 reshape.114.refs_4_
  1.9 0.0 copy-done.14
  1.9 0.6 reshape.115.refs_5_
  2.5 0.6 reshape.116.refs_6_
  3.1 0.6 reshape.117.refs_7_
  3.7 0.6 reshape.118.refs_8_
  4.3 0.6 reshape.119.refs_9_
  4.8 0.0 copy-done.19
  4.8 0.6 reshape.120.refs_10_
  5.4 0.6 reshape.121.refs_11_
  6.0 0.6 reshape.123.refs_13_
  6.6 0.0 copy-done.22
  6.6 0.6 reshape.124.refs_14_
  7.2 0.6 reshape.125.refs_15_
  7.9 0.2 copy-done.7
  8.1 0.1 copy.45
  8.2 0.1 reshape.127
  8.3 0.0 copy-start.5
  8.3 0.0 copy-start.6
  8.3 0.7 maximum_convert_fusion.refs_16_
  9.1 0.2 copy-done.5
  9.2 0.2 copy-done.6
  9.4 0.8 pad_maximum_fusion.refs_17_
  10.2 0.4 copy-done.1
  10.6 0.9 copy.49.refs_0_
  11.5 0.4 copy-done.2
  11.9 0.9 copy.50.refs_1_
  12.8 202.3 %shard_map.331 = (bf16[2,197,768]{2,1,0:T(8,128)(2,1)}, bf16[2,197,768]{2,1,0:T(8,128)(2,1)}, f32[4,2,24,384]{3,2,1,0:T(8,128)}, f32[4,96,384]{2,1,0:T(8,128)}, ...) custom-call(bf16[2,197,768]{2,1,0:T(8,128)(2,1)} %copy.49.refs_0_, bf16[2,197,768]{2,1,0:T(8,128)(2,1)} %copy.50.refs_1_, ...), custom_call_target="tpu_custom_call" | custom-call | tf_op jit(solution)/shard_map/pallas_call | solution.py:705
  215.1 2.4 %copy.57 = bf16[2,197,768]{2,0,1:T(2,128)(2,1)} copy(bf16[2,197,768]{2,1,0:T(8,128)(2,1)} %get-tuple-element.50) | data formatting | bytes 1210368
  217.5 0.0 copy-done.11
  217.5 0.6 slice_reduce_fusion
  218.1 0.6 reshape.137
  218.7 0.1 copy-done.12
  218.9 0.6 slice_reduce_fusion.6
  219.5 0.6 copy.62
  220.2 0.1 reshape.131
  220.3 0.2 copy.51
  220.4 0.8 reshape.132
  221.2 0.1 copy-done.3
  221.4 0.0 copy-start
  221.4 0.7 copy.64
  222.1 0.7 copy.63
  222.8 1.3 copy.58
  224.1 0.0 copy-done.8
  224.1 0.3 copy.56
  224.4 0.4 reshape.139
  224.8 0.6 slice.64
  (40 shorter events, 0.2 us)
Async XLA Ops:
  0.7 0.7 copy-start.13
  0.7 1.3 copy-start.14
  0.7 1.8 copy-start.15
  0.7 2.4 %copy-start.16 = (f32[768]{0:T(1024)S(1)}, f32[768]{0:T(1024)}, u32[]{:S(2)}) copy-start(f32[768]{0:T(1024)} %param.28) | copy-start | bytes 9220
  0.7 3.0 %copy-start.17 = (f32[768]{0:T(1024)S(1)}, f32[768]{0:T(1024)}, u32[]{:S(2)}) copy-start(f32[768]{0:T(1024)} %param.30) | copy-start | bytes 9220
  0.7 3.6 %copy-start.18 = (f32[768]{0:T(1024)S(1)}, f32[768]{0:T(1024)}, u32[]{:S(2)}) copy-start(f32[768]{0:T(1024)} %param.31) | copy-start | bytes 9220
  0.7 4.1 %copy-start.19 = (f32[768]{0:T(1024)S(1)}, f32[768]{0:T(1024)}, u32[]{:S(2)}) copy-start(f32[768]{0:T(1024)} %param.32) | copy-start | bytes 9220
  0.7 4.7 %copy-start.20 = (f32[768]{0:T(1024)S(1)}, f32[768]{0:T(1024)}, u32[]{:S(2)}) copy-start(f32[768]{0:T(1024)} %param.33) | copy-start | bytes 9220
  0.7 5.3 %copy-start.21 = (f32[768]{0:T(1024)S(1)}, f32[768]{0:T(1024)}, u32[]{:S(2)}) copy-start(f32[768]{0:T(1024)} %param.37) | copy-start | bytes 9220
  0.7 5.9 %copy-start.22 = (f32[768]{0:T(1024)S(1)}, f32[768]{0:T(1024)}, u32[]{:S(2)}) copy-start(f32[768]{0:T(1024)} %param.38) | copy-start | bytes 9220
  0.8 6.4 %copy-start.10 = (bf16[24,768]{1,0:T(8,128)(2,1)S(1)}, bf16[24,768]{1,0:T(8,128)(2,1)}, u32[]{:S(2)}) copy-start(bf16[24,768]{1,0:T(8,128)(2,1)} %param.29) | copy-start | bytes 110596
  5.4 1.8 copy-start.9
  7.2 0.9 copy-start.7
  8.3 0.9 copy-start.5
  8.3 1.1 copy-start.6
  9.4 1.2 copy-start.1
  10.6 1.3 copy-start.2
  215.0 2.4 %copy-start.11 = (f32[16,768]{1,0:T(8,128)S(1)}, f32[16,768]{1,0:T(8,128)}, u32[]{:S(2)}) copy-start(f32[16,768]{1,0:T(8,128)} %get-tuple-element.30) | copy-start | bytes 147460
  215.0 4.4 %copy-start.4 = (f32[4,2,24,384]{3,2,1,0:T(8,128)S(1)}, f32[4,2,24,384]{3,2,1,0:T(8,128)}, u32[]{:S(2)}) copy-start(f32[4,2,24,384]{3,2,1,0:T(8,128)} %get-tuple-element.27) | copy-start | bytes 884740
  218.1 0.7 copy-start.12
  220.3 1.1 copy-start.3
  221.4 1.5 copy-start
  222.8 1.3 copy-start.8

commit v3 on v0

--- a/solution.py
+++ b/solution.py
@@ -1,11 +1,855 @@
+import functools
+
 import jax
 import jax.numpy as jnp
 from jax import lax
+from jax.experimental import pallas as pl
+from jax.experimental.pallas import tpu as pltpu
 from jax.sharding import PartitionSpec as P
 
 EPS = 1e-06
 ROOT_HALF = 0.7071067811865476
 DENSITY = 0.3989422804014327
+
+
+MESH = pl.DeviceIdType.MESH
+F32 = jnp.float32
+BF16 = jnp.bfloat16
+TILE = 384
+PAD = 208
+TALL = 2 * PAD
+KEYS = 256
+N_COPY = 10
+NAMES = ("I0", "I1", "I2", "O", "U0", "U1", "N0", "N1")
+GATHER = {"I0": "zyx", "I1": "zxy", "I2": "zyx", "O": "zyx", "U0": "zxy", "N0": "zyx", "U1": "xzy", "N1": "zyx"}
+REDUCE = {"I0": "yxz", "I1": "yxz", "I2": "xyz", "O": "xyz", "U0": "xyz", "N0": "yzx", "U1": "yxz", "N1": "xzy"}
+ORDER = (
+    "norm1", "fill", "LI0", "LU1", "look00", "look01", "LI1", "look10", "PI0", "QI0", "LI2", "look11",
+    "look20", "PI1", "QI1", "LO", "look21", "RI0", "PI2", "turn1", "turnd", "FI0", "proj0", "RI1",
+    "QI2", "LU0", "att0", "FI1", "PO", "QO", "proj1", "att1", "RI2", "LN0", "FI2", "proj2",
+    "att2", "PU0", "QU0", "RO", "FO", "out", "PN0", "norm2", "LN1", "QN0", "RU0", "FU0",
+    "wide00", "PU1", "QU1", "wide01", "RN0", "FN0", "back00", "PN1", "back01", "QN1", "cN0", "cU0",
+    "RN1", "dN0", "RU1", "dU0", "FN1", "FU1", "wide10", "wide11", "back10", "back11", "cN1", "cU1",
+    "sec0", "eN0", "sec1", "eU0", "dN1", "dU1", "E0", "dmix", "E1", "gout", "cO", "attb0",
+    "fU0", "dO", "projb0", "fN0", "cI0", "attb1", "eN1", "dI0", "gU0", "projb1", "cI1", "attb2",
+    "eU1", "eO", "dI1", "E2", "projb2", "gN0", "cI2", "first", "eI0", "dI2", "fN1", "fU1",
+    "fO", "l0", "count0", "l1", "E3", "count1", "fI0", "count2", "eI1", "count3", "gN1", "count4",
+    "gU1", "eI2", "l2", "t0", "res", "tok", "gO", "t1", "fI1", "gI0", "fI2", "l3",
+    "t2", "gI1", "gI2", "t3",
+)
+
+
+def place():
+    dp = lax.axis_index("dp")
+    mlp = lax.axis_index("mlp")
+    return lax.div(dp, 2), lax.rem(dp, 2), lax.div(mlp, 2), lax.rem(mlp, 2)
+
+
+def device(z, x, y, c):
+    return (z * 2 + x, y * 2 + c)
+
+
+def greet(z, x, y, c):
+    barrier = pltpu.get_barrier_semaphore()
+    others = [device(lax.rem(z + d, 4), x, y, c) for d in (1, 2, 3)]
+    others += [device(z, 1 - x, y, c), device(z, x, 1 - y, c), device(z, 1 - x, 1 - y, c), device(z, x, y, 1 - c)]
+    for other in others:
+        pl.semaphore_signal(barrier, inc=1, device_id=other, device_id_type=MESH)
+    pl.semaphore_wait(barrier, len(others))
+
+
+class Link:
+    def __init__(self, send, recv):
+        self.send, self.recv, self.pending = send, recv, {}
+
+    def copy(self, src, dst, slot, target, group=None):
+        made = pltpu.make_async_remote_copy(
+            src_ref=src,
+            dst_ref=dst,
+            send_sem=self.send.at[slot],
+            recv_sem=self.recv.at[slot],
+            device_id=target,
+            device_id_type=MESH,
+        )
+        made.start()
+        self.pending.setdefault(group, []).append(made)
+        return made
+
+    def drain(self, *groups):
+        for group in groups or tuple(self.pending):
+            for made in self.pending.pop(group, []):
+                made.wait_send()
+
+
+class Unit:
+    def __init__(self, link, ref, name, where, base):
+        self.link, self.ref, self.where, self.base, self.name = link, ref, where, base, name
+        self.narrow = name[0] in "IO"
+        self.group = name if base < 8 * N_COPY else None
+
+    def put(self, src, dst, slot, target):
+        return self.link.copy(src, dst, self.base + slot, target, self.group)
+
+    def block(self, z, x, y, c):
+        return self.ref.at[c, z, x, y] if self.narrow else self.ref.at[y, c, z, x]
+
+    def line(self, x, y, c):
+        return self.ref.at[c, :, x, y] if self.narrow else self.ref.at[y, c, :, x]
+
+    def by_core(self, c):
+        return self.ref.at[c] if self.narrow else self.ref.at[:, c]
+
+    def by_y(self, y, c):
+        return self.ref.at[c, :, :, y] if self.narrow else self.ref.at[y, c]
+
+    def by_x(self, x, c):
+        return self.ref.at[c, :, x] if self.narrow else self.ref.at[:, c, :, x]
+
+    def along_y(self, z, x, c):
+        return self.ref.at[c, z, x] if self.narrow else self.ref.at[:, c, z, x]
+
+    def along_x(self, z, y, c):
+        return self.ref.at[c, z, :, y] if self.narrow else self.ref.at[y, c, z]
+
+    def spread(self, part, slot):
+        z, x, y, c = self.where
+        return [self.put(part, part, slot + d - 1, device(lax.rem(z + d, 4), x, y, c)) for d in (1, 2, 3)]
+
+    def across(self, axis, src, dst, slot):
+        z, x, y, c = self.where
+        target = {"x": (z, 1 - x, y, c), "y": (z, x, 1 - y, c), "c": (z, x, y, 1 - c)}[axis]
+        return self.put(src, dst, slot, device(*target))
+
+
+class Gather(Unit):
+    def Z(self):
+        self.z = self.spread(self.block(*self.where), 0)
+
+    def L(self):
+        z, x, y, c = self.where
+        for made in self.z:
+            made.wait_recv()
+        part = self.line(x, y, c)
+        self.made = {axis: self.across(axis, part, part, 3 + n) for n, axis in enumerate(GATHER[self.name][1:] + "c")}
+        self.to_c = [self.made["c"]]
+
+    def pass_on(self, axis, slot):
+        z, x, y, c = self.where
+        self.made[axis].wait_recv()
+        part = self.line(1 - x, y, c) if axis == "x" else self.line(x, 1 - y, c)
+        self.to_c.append(self.across("c", part, part, slot))
+        return part
+
+    def P(self):
+        first, last = GATHER[self.name][1:]
+        part = self.pass_on(first, 6)
+        self.last = self.across(last, part, part, 7)
+
+    def Q(self):
+        self.pass_on(GATHER[self.name][2], 8)
+
+    def R(self):
+        z, x, y, c = self.where
+        self.last.wait_recv()
+        part = self.line(1 - x, 1 - y, c)
+        self.to_c.append(self.across("c", part, part, 9))
+
+    def F(self):
+        for made in self.to_c:
+            made.wait_recv()
+
+
+class GatherZ(Unit):
+    def Z(self):
+        part = self.block(*self.where)
+        self.first = self.across(GATHER[self.name][0], part, part, 0)
+        self.z = self.spread(part, 1)
+
+    def L(self):
+        z, x, y, c = self.where
+        self.first.wait_recv()
+        part = self.block(z, 1 - x, y, c) if GATHER[self.name][0] == "x" else self.block(z, x, 1 - y, c)
+        self.z += self.spread(part, 4)
+
+    def P(self):
+        z, x, y, c = self.where
+        for made in self.z:
+            made.wait_recv()
+        last = GATHER[self.name][2]
+        part = self.by_x(x, c) if last == "x" else self.by_y(y, c)
+        self.last = self.across(last, part, part, 7)
+        self.to_c = [self.across("c", part, part, 8)]
+
+    def Q(self):
+        pass
+
+    def R(self):
+        z, x, y, c = self.where
+        self.last.wait_recv()
+        part = self.by_x(1 - x, c) if GATHER[self.name][2] == "x" else self.by_y(1 - y, c)
+        self.to_c.append(self.across("c", part, part, 9))
+
+    def F(self):
+        for made in self.to_c:
+            made.wait_recv()
+
+
+def mix(here, *there):
+    total = here[...].astype(F32)
+    for other in there:
+        total = total + other[...].astype(F32)
+    here[...] = total.astype(BF16)
+
+
+class Reduce(Unit):
+    def set_buffers(self, half, quarter, third, fourth):
+        self.half, self.quarter, self.third, self.fourth = half, quarter, third, fourth
+
+    @staticmethod
+    def buffers(name):
+        rows = 48 if name[0] in "IO" else 96
+        half = (4, 2, 2, rows, TILE) if name[0] in "IO" else (2, 4, 2, rows, TILE)
+        pair = (2, 4) if name[0] not in "IO" and REDUCE[name][0] == "x" else (4, 2)
+        if REDUCE[name][2] == "z":
+            return (half, (*pair, rows, TILE), (4, rows, TILE), (3, rows, TILE))
+        return (half, (*pair, rows, TILE), (3, 2, rows, TILE), (rows, TILE))
+
+    def c(self):
+        z, x, y, c = self.where
+        self.made = self.across("c", self.by_core(1 - c), self.half, 0)
+
+    def d(self):
+        z, x, y, c = self.where
+        self.made.wait_recv()
+        mix(self.by_core(c), self.half)
+        first = REDUCE[self.name][0]
+        self.made = self.across(first, self.by_x(1 - x, c) if first == "x" else self.by_y(1 - y, c), self.quarter, 1)
+
+    def e(self):
+        z, x, y, c = self.where
+        self.made.wait_recv()
+        mix(self.by_x(x, c) if REDUCE[self.name][0] == "x" else self.by_y(y, c), self.quarter)
+        last = REDUCE[self.name][1]
+        self.made = self.across(last, self.line(1 - x, y, c) if last == "x" else self.line(x, 1 - y, c), self.third, 2)
+
+    def f(self):
+        z, x, y, c = self.where
+        self.made.wait_recv()
+        mix(self.line(x, y, c), self.third)
+        self.z = []
+        for d in (1, 2, 3):
+            far = lax.rem(z + d, 4)
+            self.z.append(self.put(self.block(far, x, y, c), self.fourth.at[d - 1], 2 + d, device(far, x, y, c)))
+
+    def total(self):
+        for made in self.z:
+            made.wait_recv()
+        total = self.block(*self.where)[...].astype(F32)
+        for d in range(3):
+            total = total + self.fourth[d].astype(F32)
+        return total
+
+
+class ReduceZ(Reduce):
+    def pair(self, z):
+        x, y, c = self.where[1:]
+        return self.along_y(z, x, c) if REDUCE[self.name][0] == "x" else self.along_x(z, y, c)
+
+    def e(self):
+        z, x, y, c = self.where
+        self.made.wait_recv()
+        mix(self.by_x(x, c) if REDUCE[self.name][0] == "x" else self.by_y(y, c), self.quarter)
+        self.z = []
+        for d in (1, 2, 3):
+            far = lax.rem(z + d, 4)
+            self.z.append(self.put(self.pair(far), self.third.at[d - 1], 2 + d, device(far, x, y, c)))
+
+    def f(self):
+        z, x, y, c = self.where
+        for made in self.z:
+            made.wait_recv()
+        mix(self.pair(z), *(self.third.at[d] for d in range(3)))
+        last = REDUCE[self.name][2]
+        part = self.block(z, 1 - x, y, c) if last == "x" else self.block(z, x, 1 - y, c)
+        self.made = self.across(last, part, self.fourth, 6)
+
+    def total(self):
+        self.made.wait_recv()
+        return self.block(*self.where)[...].astype(F32) + self.fourth[...].astype(F32)
+
+
+class Everywhere:
+    def __init__(self, link, ref, core_ref, plane_ref, line_ref, base, where):
+        self.link, self.ref, self.where, self.base = link, ref, where, base
+        self.core_ref, self.plane_ref, self.line_ref = core_ref, plane_ref, line_ref
+
+    def to_core(self):
+        z, x, y, c = self.where
+        self.made = [self.link.copy(self.ref, self.core_ref, self.base, device(z, x, y, 1 - c))]
+
+    def wait(self):
+        for made in self.made:
+            made.wait_recv()
+
+    def to_plane(self):
+        z, x, y, c = self.where
+        self.wait()
+        chip = self.plane_ref.at[3]
+        chip[...] = self.ref[...] + self.core_ref[...]
+        targets = (device(z, 1 - x, y, c), device(z, x, 1 - y, c), device(z, 1 - x, 1 - y, c))
+        self.made = [
+            self.link.copy(chip, self.plane_ref.at[n], self.base + 1 + n, target) for n, target in enumerate(targets)
+        ]
+
+    def to_line(self):
+        z, x, y, c = self.where
+        self.wait()
+        got = self.plane_ref
+        self.line_ref[z] = (got[3] + got[0]) + (got[1] + got[2])
+        part = self.line_ref.at[z]
+        self.made = [
+            self.link.copy(part, part, self.base + 3 + d, device(lax.rem(z + d, 4), x, y, c)) for d in (1, 2, 3)
+        ]
+
+    def total(self):
+        self.wait()
+        got = self.line_ref
+        return (got[0] + got[1]) + (got[2] + got[3])
+
+
+def dot(left, right):
+    return lax.dot_general(left, right, (((1,), (0,)), ((), ())), preferred_element_type=F32)
+
+
+def dot_nt(left, right):
+    return lax.dot_general(left, right, (((1,), (1,)), ((), ())), preferred_element_type=F32)
+
+
+def dot_tn(left, right):
+    return lax.dot_general(left, right, (((0,), (0,)), ((), ())), preferred_element_type=F32)
+
+
+def fold(values):
+    rows, width = values.shape
+    return jnp.sum(values.reshape(rows // 8, 8, width), 0)
+
+
+def unit_of(values):
+    mean = jnp.mean(values, -1, keepdims=True)
+    centred = values - mean
+    variance = jnp.mean(centred * centred, -1, keepdims=True)
+    scaled = lax.rsqrt(variance + EPS)
+    return centred * scaled, scaled
+
+
+def loop(count, step, init):
+    return lax.fori_loop(0, count, step, init)
+
+
+def by_rows(step, init, first=0, count=13):
+    size = 32
+
+    def one(index, carried):
+        return step(pl.ds(pl.multiple_of((index + first) * size, size), size), carried)
+
+    one.__name__ = step.__name__
+    return loop(count, one, init)
+
+
+def layer_kernel(*refs):
+    (
+        tokens, keep, places, cotangent, first_gain1, first_shift1, inner_in, query_bias1, value_bias1, outer_in, outer_bias1,
+        attend_scale1, second_gain1, second_shift1, up_in, up_bias, down_in, down_bias1, feed_scale1, table_in,
+        result, token_grad, inner_out, outer_out, up_out, down_out, early_out, late_out, table_out,
+        *rest,
+    ) = refs
+    (
+        narrow, wide, small, pair, swap,
+        source, upstream, normed1, normed1_t, normed2, normed2_t, qkv, bias, mask, index, probs, mix_t, attend, resid,
+        dfeed, dfeed_t, hidden, slope, total, dnormed2, shifts, ups, tab, vectors,
+        early, late, hits, early_core, early_plane, early_line, late_core, late_plane, late_line, hits_core, hits_plane, hits_line,
+        send, recv, *buffers,
+    ) = rest
+    dresid, dproj, dmixed, mixed, dattend = resid, hidden, normed2, normed2, dfeed
+    where = z, x, y, c = place()
+    link = Link(send, recv)
+    gathers, reduces = {}, {}
+    for n, name in enumerate(NAMES):
+        ref = narrow.at[n] if n < 4 else wide.at[n - 4]
+        kind = Gather if GATHER[name][0] == "z" else GatherZ
+        gathers[name] = kind(link, ref, name, where, n * N_COPY)
+        kind = Reduce if REDUCE[name][2] == "z" else ReduceZ
+        reduces[name] = kind(link, ref, name, where, (8 + n) * N_COPY)
+        reduces[name].set_buffers(*buffers[4 * n : 4 * n + 4])
+    spare = 16 * N_COPY
+    sums = {
+        "E": Everywhere(link, early, early_core, early_plane, early_line, spare + 5, where),
+        "l": Everywhere(link, late, late_core, late_plane, late_line, spare + 15, where),
+        "t": Everywhere(link, hits, hits_core, hits_plane, hits_line, spare + 25, where),
+    }
+    mates = []
+    kept = {}
+    for k in range(3):
+        for core in range(2):
+            for part in range(3):
+                start = part * 768 + (core * 3 + k) * 128
+                small[k, core, :, part * 128 : part * 128 + 128] = inner_in[:, start : start + 128].astype(F32)
+    for core in range(2):
+        small[3, core] = outer_in[:, core * TILE : core * TILE + TILE].astype(F32)
+    for k in range(2):
+        cols = slice(k * TILE, k * TILE + TILE)
+        wide[k, y, c, z, x] = up_in[:, cols]
+        wide[2 + k, y, c, z, x] = down_in[:, cols]
+    greet(*where)
+    mate = link.copy(small.at[:, 1 - c], pair.at[:, c], spare, device(z, x, y, 1 - c))
+    for name in NAMES[4:]:
+        if GATHER[name][0] != "z":
+            gathers[name].Z()
+    pair[:, c] = small[:, c]
+    mate.wait_recv()
+    link.drain(None)
+    for unit in range(4):
+        narrow[unit, c, z, x, y] = pair[unit].reshape(48, TILE).astype(BF16)
+    for name in GATHER:
+        if name[0] in "IO" or GATHER[name][0] == "z":
+            gathers[name].Z()
+
+    given = (first_gain1, first_shift1, query_bias1, value_bias1, outer_bias1, attend_scale1, second_gain1, second_shift1, down_bias1, feed_scale1)
+    for n, ref in enumerate(given):
+        vectors[n] = ref[...].reshape(1, 768)
+    (first_gain, first_shift, query_bias, value_bias, outer_bias, attend_scale, second_gain, second_shift, down_bias, feed_scale) = (
+        vectors.at[n] for n in range(10)
+    )
+
+    for image in range(2):
+        last = pl.ds(image * PAD + 192, 16)
+        source[last, :] = jnp.zeros((16, 768), BF16)
+        upstream[last, :] = jnp.zeros((16, 768), BF16)
+        source[pl.ds(image * PAD, 197), :] = tokens[image]
+        upstream[pl.ds(image * PAD, 197), :] = cotangent[image]
+    zero = jnp.zeros((8, 768), F32)
+    lane = lax.broadcasted_iota(jnp.int32, (1, 128), 1)
+    picks = [(lane < 64).astype(F32).astype(BF16), (lane >= 64).astype(F32).astype(BF16)]
+
+    def rows_of(image):
+        return slice(image * PAD, image * PAD + PAD)
+
+    def keys_of(image):
+        return slice(image * PAD, image * PAD + KEYS)
+
+    def cols_of(p):
+        return pl.ds(pl.multiple_of(p * 128, 128), 128)
+
+    def half(core):
+        return slice(core * TILE, core * TILE + TILE)
+
+    def norm1():
+        def norm_first(rows, carried):
+            unit, _ = unit_of(source[rows, :].astype(F32))
+            normed1[rows, :] = (unit * first_gain[...] + first_shift[...]).astype(BF16)
+            lifted = upstream[rows, :].astype(F32) * feed_scale[...]
+            dfeed[rows, :] = lifted.astype(BF16)
+            return carried + fold(lifted)
+
+        early[...] = jnp.zeros((16, 768), F32)
+        late[...] = jnp.zeros((8, 768), F32)
+        early[4:5, :] = jnp.sum(by_rows(norm_first, zero), 0, keepdims=True)
+        zero_row = jnp.zeros((1, 128), F32)
+        for p in range(6):
+            cols = slice(p * 128, p * 128 + 128)
+            shifts[p] = jnp.concatenate([query_bias[:, cols], zero_row, value_bias[:, cols]], axis=1)
+            qkv[p, TALL:, :] = jnp.zeros((48, TILE), BF16)
+
+    def fill():
+        index[...] = jnp.full((PAD, KEYS), -1, jnp.int32)
+        index[0:197, 0:197] = places[...]
+        tab[...] = jnp.zeros((12, 1, 768), F32)
+        for head in range(12):
+            tab[head, :, 0:732] = table_in[head : head + 1, :]
+        row_of = lax.broadcasted_iota(jnp.int32, (PAD, KEYS), 0)
+        col_of = lax.broadcasted_iota(jnp.int32, (PAD, KEYS), 1)
+        for image in range(2):
+            mask[image] = jnp.full((PAD, KEYS), -1e30, F32)
+            shown = jnp.where(keep[image : image + 1, :] == 1, 0.0, -1e30).astype(F32)
+            mask[image, :, 0:197] = jnp.broadcast_to(shown, (PAD, 197))
+            mask[image] = jnp.where(row_of == col_of, 0.0, mask[image])
+
+    def look(k, core):
+        def look_up(t, carried):
+            head = 2 * (core * 3 + k) + t
+            for side in range(2):
+                cols = slice(side * 128, side * 128 + 128)
+                spot = index[:, cols]
+                low, high = spot & 127, spot >> 7
+                found = jnp.zeros((PAD, 128), F32)
+                for piece in range(6):
+                    row = tab[head, :, piece * 128 : piece * 128 + 128]
+                    picked = jnp.take_along_axis(jnp.broadcast_to(row, (PAD, 128)), low, axis=1)
+                    found = jnp.where(high == piece, picked, found)
+                bias[head, :, cols] = found
+            return carried
+
+        loop(2, look_up, 0)
+
+    def turn1():
+        normed1_t[...] = normed1[...].T
+
+    def turnd():
+        dfeed_t[...] = dfeed[...].T
+
+    def proj(k):
+        def project(core, carried):
+            p = core * 3 + k
+            weight = narrow[k, core].reshape(768, TILE)
+            scaling = jnp.where(lax.broadcasted_iota(jnp.int32, (1, TILE), 1) < 128, 0.125, 1.0).astype(F32)
+            value = (dot(normed1[...], weight) + shifts[p]).astype(BF16)
+            qkv[p, 0:TALL, :] = (value.astype(F32) * scaling).astype(BF16)
+            return carried
+
+        loop(2, project, 0)
+
+    def att(k):
+        def attend_pair(core, carried):
+            p = core * 3 + k
+            first_half = lax.broadcasted_iota(jnp.int32, (PAD, 128), 1) < 64
+            for image in range(2):
+                query = qkv[p, rows_of(image), 0:128]
+                keys = qkv[p, keys_of(image), 128:256]
+                values = qkv[p, keys_of(image), 256:384]
+                outs = []
+                for t in range(2):
+                    logits = dot_nt(query * picks[t], keys) + bias[2 * p + t] + mask[image]
+                    top = jnp.max(logits, -1, keepdims=True)
+                    expd = jnp.exp(logits - top)
+                    share = (expd * (1.0 / jnp.sum(expd, -1, keepdims=True))).astype(BF16)
+                    probs[image, 2 * p + t] = share
+                    outs.append(dot(share, values))
+                mixed[rows_of(image), cols_of(p)] = jnp.where(first_half, outs[0], outs[1]).astype(BF16)
+            return carried
+
+        loop(2, attend_pair, 0)
+
+    def out():
+        for core in range(2):
+            attend[:, half(core)] = dot(mixed[...], narrow[3, core].reshape(768, TILE)) + outer_bias[:, half(core)]
+        mix_t[...] = mixed[...].T
+
+    def norm2():
+        def norm_second(rows, carried):
+            value = source[rows, :].astype(F32) + attend_scale[...] * attend[rows, :]
+            resid[rows, :] = value
+            unit, _ = unit_of(value)
+            normed2[rows, :] = (unit * second_gain[...] + second_shift[...]).astype(BF16)
+            return carried
+
+        by_rows(norm_second, 0)
+        normed2_t[...] = normed2[...].T
+
+    def widening(k, side):
+        def widen(core, carried):
+            weight = wide[k, side, core].reshape(768, TILE)
+            cols = pl.ds(pl.multiple_of((side * 2 + core) * 768 + k * TILE, 128), TILE)
+            pre = dot(normed2[...], weight) + up_bias[:, cols]
+            cumul = 0.5 * (1.0 + lax.erf(pre * ROOT_HALF))
+            b = k * 4 + side * 2 + core
+            hidden[b] = (pre * cumul).astype(BF16)
+            slope[b] = (cumul + pre * jnp.exp(-0.5 * pre * pre) * DENSITY).astype(BF16)
+            return carried
+
+        loop(2, widen, 0)
+
+    def back(k, side):
+        if side == 0:
+            link.drain("U" + str(k), "N" + str(k))
+        b = k * 4 + side * 2
+
+        def narrow_back(step, carried):
+            down = jnp.concatenate([wide[2 + k, side, core].reshape(768, TILE) for core in range(2)], axis=1)
+            up = jnp.concatenate([wide[k, side, core].reshape(768, TILE) for core in range(2)], axis=1)
+            both = jnp.concatenate([hidden[b], hidden[b + 1]], axis=1)
+            part = dot_nt(both, down)
+            total[...] = part if b == 0 else total[...] + part
+            tilt = jnp.concatenate([slope[b], slope[b + 1]], axis=1).astype(F32)
+            dpre = (dot(dfeed[...], down) * tilt).astype(BF16)
+            ups[b // 2] = jnp.sum(fold(dpre.astype(F32)), 0, keepdims=True)
+            part = dot_nt(dpre, up)
+            dnormed2[...] = part if b == 0 else dnormed2[...] + part
+            up_grad = dot(normed2_t[...], dpre).astype(BF16)
+            down_grad = dot(dfeed_t[...], both).astype(BF16)
+            for core in range(2):
+                wide[2 + k, side, core] = up_grad[:, half(core)].reshape(4, 2, 96, TILE)
+                wide[k, side, core] = down_grad[:, half(core)].reshape(4, 2, 96, TILE)
+            return carried
+
+        loop(1, narrow_back, 0)
+
+    def sec(n):
+        def second_back(rows, carried):
+            feed_scale_sum, gain_sum, shift_sum, scale_sum, bias_sum = carried
+            feed = total[rows, :] + down_bias[...]
+            above = upstream[rows, :].astype(F32)
+            value = resid[rows, :]
+            total[rows, :] = value + feed_scale[...] * feed
+            unit, scaled = unit_of(value)
+            grad = dnormed2[rows, :]
+            inner = grad * second_gain[...]
+            first = jnp.mean(inner, -1, keepdims=True)
+            second = jnp.mean(inner * unit, -1, keepdims=True)
+            back = above + scaled * (inner - first - unit * second)
+            dresid[rows, :] = back
+            lifted = attend_scale[...] * back
+            dattend[rows, :] = lifted.astype(BF16)
+            return (
+                feed_scale_sum + fold(feed * above),
+                gain_sum + fold(grad * unit),
+                shift_sum + fold(grad),
+                scale_sum + fold(attend[rows, :] * back),
+                bias_sum + fold(lifted),
+            )
+
+        kept["sec"] = by_rows(second_back, kept.get("sec", (zero,) * 5), 7 * n, 7 - n)
+        if n == 1:
+            for block in range(4):
+                for k in range(2):
+                    b = k * 4 + block
+                    early[8 + block : 9 + block, half(k)] = ups[b // 2, :, half(b % 2)]
+            for row, value in zip((5, 2, 3, 1, 0), kept.pop("sec")):
+                early[row : row + 1, :] = jnp.sum(value, 0, keepdims=True)
+
+    def res():
+        for image in range(2):
+            result[image] = total[pl.ds(image * PAD, 197), :].astype(BF16)
+        kept["res"] = True
+
+    def dmix():
+        parts = [dot_nt(dattend[:, half(core)], narrow[3, core].reshape(768, TILE)) for core in range(2)]
+        dmixed[...] = (parts[0] + parts[1]).astype(BF16)
+
+    def gout():
+        link.drain("O")
+        for core in range(2):
+            narrow[3, core] = dot(mix_t[...], dattend[:, half(core)]).astype(BF16).reshape(4, 2, 2, 48, TILE)
+
+    def attb(k):
+        def attend_back(core, carried):
+            p = core * 3 + k
+            first_half = lax.broadcasted_iota(jnp.int32, (PAD, 128), 1) < 64
+            hit = [None, None]
+            for image in range(2):
+                rows = rows_of(image)
+                query = qkv[p, rows, 0:128]
+                keys = qkv[p, keys_of(image), 128:256]
+                values = qkv[p, keys_of(image), 256:384]
+                above = dmixed[rows, cols_of(p)]
+                dquery, dkeys, dvalues = [], [], []
+                for t in range(2):
+                    share = probs[image, 2 * p + t]
+                    dvalues.append(dot_tn(share, above)[0:PAD])
+                    dshare = dot_nt(above * picks[t], values)
+                    full = share.astype(F32)
+                    dlogits = full * (dshare - jnp.sum(dshare * full, -1, keepdims=True))
+                    hit[t] = dlogits if image == 0 else hit[t] + dlogits
+                    low = dlogits.astype(BF16)
+                    dquery.append(dot(low, keys) * 0.125)
+                    dkeys.append(dot_tn(low, query)[0:PAD])
+                dproj[p, rows, 0:128] = jnp.where(first_half, dquery[0], dquery[1]).astype(BF16)
+                dproj[p, rows, 128:256] = jnp.where(first_half, dkeys[0], dkeys[1]).astype(BF16)
+                dproj[p, rows, 256:384] = jnp.where(first_half, dvalues[0], dvalues[1]).astype(BF16)
+            for t in range(2):
+                bias[2 * p + t] = hit[t]
+            return carried
+
+        loop(2, attend_back, 0)
+
+    def projb(k):
+        link.drain("I" + str(k))
+
+        def project_back(core, carried):
+            p = core * 3 + k
+            grad = dproj[p]
+            summed = jnp.sum(fold(grad.astype(F32)), 0, keepdims=True)
+            late[2:3, cols_of(p)] = summed[:, 0:128]
+            late[3:4, cols_of(p)] = summed[:, 256:384]
+            part = dot_nt(grad, narrow[k, core].reshape(768, TILE))
+            dnormed2[...] = jnp.where(core == 0, 0.0, dnormed2[...]) + part if k == 0 else dnormed2[...] + part
+            narrow[k, core] = dot(normed1_t[...], grad).astype(BF16).reshape(4, 2, 2, 48, TILE)
+            return carried
+
+        loop(2, project_back, 0)
+
+    def first():
+        def first_back(rows, carried):
+            gain_sum, shift_sum = carried
+            grad = dnormed2[rows, :]
+            unit, scaled = unit_of(source[rows, :].astype(F32))
+            inner = grad * first_gain[...]
+            mean = jnp.mean(inner, -1, keepdims=True)
+            second = jnp.mean(inner * unit, -1, keepdims=True)
+            dresid[rows, :] = dresid[rows, :] + scaled * (inner - mean - unit * second)
+            return gain_sum + fold(grad * unit), shift_sum + fold(grad)
+
+        found = by_rows(first_back, (zero, zero))
+        late[0:1, :] = jnp.sum(found[0], 0, keepdims=True)
+        late[1:2, :] = jnp.sum(found[1], 0, keepdims=True)
+
+    def tok():
+        for image in range(2):
+            token_grad[image] = dresid[pl.ds(image * PAD, 197), :].astype(BF16)
+
+    def counting(n):
+        low_of = lax.broadcasted_iota(jnp.int32, (128, KEYS), 0)
+        high_of = lax.broadcasted_iota(jnp.int32, (8, KEYS), 0)
+
+        def count(group, carried):
+            eight = pl.ds(pl.multiple_of((group + 5 * n) * 8, 8), 8)
+            spots = index[eight, :]
+            for r in range(8):
+                spot = jnp.broadcast_to(spots[r : r + 1, :], (8, KEYS))
+                high = (spot >> 7) == high_of
+                parts = []
+                for head in range(12):
+                    grads = bias[head, eight, :]
+                    parts.append(jnp.where(high, jnp.broadcast_to(grads[r : r + 1, :], (8, KEYS)), 0.0))
+                spread = jnp.concatenate(parts, axis=0).astype(BF16)
+                low = jnp.concatenate([spot & 127] * 16, axis=0)
+                which = (low == low_of).astype(F32).astype(BF16)
+                carried = carried + dot_nt(spread, which)
+            return carried
+
+        before = jnp.zeros((96, 128), F32) if n == 0 else hits[...]
+        hits[...] = loop(5, count, before)
+
+    def settle(name):
+        value = reduces[name].total()
+        n = NAMES.index(name)
+        if n < 4:
+            small[n] = value.reshape(2, 24, TILE)
+            swap[n, c] = small[n, c]
+            mates.append(link.copy(small.at[n, 1 - c], swap.at[n, c], spare + 1 + n, device(z, x, y, 1 - c)))
+        elif n < 6:
+            down_out[:, half(n - 4)] = value
+        else:
+            up_out[:, half(n - 6)] = value
+
+    steps = {"norm1": norm1, "fill": fill, "turn1": turn1, "turnd": turnd, "out": out, "norm2": norm2, "dmix": dmix, "gout": gout, "first": first, "res": res, "tok": tok}
+    for k in range(3):
+        steps["proj" + str(k)] = functools.partial(proj, k)
+        steps["att" + str(k)] = functools.partial(att, k)
+        steps["attb" + str(k)] = functools.partial(attb, k)
+        steps["projb" + str(k)] = functools.partial(projb, k)
+        for i in range(2):
+            steps["look" + str(k) + str(i)] = functools.partial(look, k, i)
+    for i in range(2):
+        steps["sec" + str(i)] = functools.partial(sec, i)
+        for k in range(2):
+            steps["wide" + str(k) + str(i)] = functools.partial(widening, k, i)
+            steps["back" + str(k) + str(i)] = functools.partial(back, k, i)
+    for n in range(5):
+        steps["count" + str(n)] = functools.partial(counting, n)
+    for name in NAMES:
+        for event in "LPQRF":
+            steps[event + name] = getattr(gathers[name], event)
+        for event in "cdef":
+            steps[event + name] = getattr(reduces[name], event)
+        steps["g" + name] = functools.partial(settle, name)
+    for what, everywhere in sums.items():
+        steps[what + "0"] = everywhere.to_core
+        steps[what + "1"] = everywhere.to_plane
+        steps[what + "2"] = everywhere.to_line
+
+    def give(what, ref):
+        ref[...] = sums[what].total()
+
+    steps["E3"] = functools.partial(give, "E", early_out)
+    steps["l3"] = functools.partial(give, "l", late_out)
+
+    def give_table():
+        found = sums["t"].total().reshape(12, 8, 128)
+        for piece in range(6):
+            width = min(128, 732 - piece * 128)
+            table_out[:, piece * 128 : piece * 128 + width] = found[:, piece, 0:width]
+
+    steps["t3"] = give_table
+    for name in ORDER:
+        steps[name]()
+    for made in mates:
+        made.wait_recv()
+    for k in range(3):
+        for core in range(2):
+            for part in range(3):
+                start = part * 768 + (core * 3 + k) * 128
+                inner_out[:, start : start + 128] = swap[k, core, :, part * 128 : part * 128 + 128]
+    for core in range(2):
+        outer_out[:, half(core)] = swap[3, core]
+    link.drain()
+
+
+def run_layer(*operands):
+    def vmem(*shape, dtype=BF16):
+        return pltpu.VMEM(shape, dtype)
+
+    scratch = [
+        vmem(4, 2, 4, 2, 2, 48, TILE),
+        vmem(4, 2, 2, 4, 2, 96, TILE),
+        vmem(4, 2, 24, TILE, dtype=F32),
+        vmem(4, 2, 24, TILE, dtype=F32),
+        vmem(4, 2, 24, TILE, dtype=F32),
+        vmem(TALL, 768),
+        vmem(TALL, 768),
+        vmem(TALL, 768),
+        vmem(768, TALL),
+        vmem(TALL, 768),
+        vmem(768, TALL),
+        vmem(6, TALL + 48, TILE),
+        vmem(12, PAD, KEYS, dtype=F32),
+        vmem(2, PAD, KEYS, dtype=F32),
+        vmem(PAD, KEYS, dtype=jnp.int32),
+        vmem(2, 12, PAD, KEYS),
+        vmem(768, TALL),
+        vmem(TALL, 768, dtype=F32),
+        vmem(TALL, 768, dtype=F32),
+        vmem(TALL, 768),
+        vmem(768, TALL),
+        vmem(8, TALL, TILE),
+        vmem(8, TALL, TILE),
+        vmem(TALL, 768, dtype=F32),
+        vmem(TALL, 768, dtype=F32),
+        vmem(6, 1, TILE, dtype=F32),
+        vmem(4, 1, 768, dtype=F32),
+        vmem(12, 1, 768, dtype=F32),
+        vmem(10, 1, 768, dtype=F32),
+        vmem(16, 768, dtype=F32),
+        vmem(8, 768, dtype=F32),
+        vmem(96, 128, dtype=F32),
+    ]
+    for shape in ((16, 768), (8, 768), (96, 128)):
+        scratch += [vmem(*shape, dtype=F32), vmem(4, *shape, dtype=F32), vmem(4, *shape, dtype=F32)]
+    copies = 16 * N_COPY + 40
+    scratch += [pltpu.SemaphoreType.DMA((copies,)), pltpu.SemaphoreType.DMA((copies,))]
+    for name in NAMES:
+        scratch += [vmem(*shape) for shape in Reduce.buffers(name)]
+    shapes = [((2, 197, 768), BF16), ((2, 197, 768), BF16), ((24, 2304), F32), ((24, 768), F32), ((96, 768), F32), ((96, 768), F32)]
+    shapes += [((16, 768), F32), ((8, 768), F32), ((12, 732), F32)]
+    return pl.pallas_call(
+        layer_kernel,
+        out_shape=[jax.ShapeDtypeStruct(*shape) for shape in shapes],
+        in_specs=[pl.BlockSpec(memory_space=pltpu.VMEM)] * len(operands),
+        out_specs=[pl.BlockSpec(memory_space=pltpu.VMEM)] * len(shapes),
+        scratch_shapes=scratch,
+        compiler_params=pltpu.CompilerParams(
+            collective_id=0, has_side_effects=True, vmem_limit_bytes=62 * 2**20
+        ),
+    )(*operands)
+
+
+def fast_body(*operands):
+    operands = list(operands)
+    operands[15] = operands[15].reshape(1, -1)
+    operands[16] = operands[16].T
+    operands[19] = operands[19].T
+    result, token_grad, inner, outer, up, down, early, late, table = run_layer(*operands)
+    first = (result, token_grad, inner, outer, up, down.T, late[0], late[1], late[2], late[3])
+    return (*first, early[0], early[1], early[2], early[3], early[8:12].reshape(3072), early[4], early[5], table.T)
 
 
 def layer_norm(values, gain, shift):
@@ -276,6 +1120,7 @@
 
 
 def solution(mesh):
+    special = mesh.shape["dp"] == 8 and mesh.shape["mlp"] == 4
     placed = (
         P(None, ("dp", "mlp"), None),
         P(None, ("dp", "mlp")),
@@ -299,7 +1144,7 @@
         P(),
     )
     return jax.shard_map(
-        body,
+        fast_body if special else body,
         mesh=mesh,
         in_specs=placed,
         out_specs=(

time: 1440 us -> 182 us (0.13)
  waiting for transfers between devices: 580 us -> 0 us
  other arithmetic: 441 us -> 0 us
  local copies, waits for them, and re-layouts: 257 us -> 12.7 us
  Pallas kernels: 0 us -> 168 us
  matrix products: 83.5 us -> 0 us
  blocking collectives: 46.6 us -> 0 us
  between operations: 16 us -> 0.7 us
    scatter-add x2 -> x0, other arithmetic: 415 us -> none  [body(): sum_table_heads.at[:, flat_index].add(dlogits.reshape(heads, rows * rows))]
    reduce_scatter x4 -> x0, waiting for transfers between devices: 375 us -> none  [the longest x1 125 us: body(): lax.psum_scatter(sum_inner, ('dp', 'mlp'), scatter_dimension=0, tiled=True)]
    pallas_call x0 -> x1, Pallas kernels: none -> 168 us  [run_layer(): pl.pallas_call(layer_kernel, out_shape=[jax.ShapeDtypeStruct(*shape) for...]
    gather x4 -> x0, local copies, waits for them, and re-layouts: 145 us -> none  [body(): bias = table_by_head[:, position_index]]
    psum x1 -> x0, waiting for transfers between devices: 103 us -> none  [body(): lax.psum((sum_first_gain, sum_first_shift, sum_query_bias, sum_value_bias...]
    all_gather x8 -> x0, waiting for transfers between devices: 99.2 us -> none  [the longest x1 40.6 us: fetch(): lax.all_gather(up_weight, 'dp', axis=0, tiled=True)]
    dot_general x36 -> x0, matrix products: 83.5 us -> none  [the longest x8 24.6 us: contract_rows(): lax.dot_general(left, right, (((0,), (0,)), ((), ())), preferred_element_...]
    unnamed x238 -> x27, local copies, waits for them, and re-layouts: 60.9 us -> 11.4 us
  transfers between devices with their start and end apart: 17 -> 0, of which waited for: 9 -> 0; matrix products, arithmetic and copies ran while one was open for 18% -> 0% of each run, Pallas kernels for 0% -> 0%
where the time goes in v3:
time: 182 us
  Pallas kernels  168 us (92%)
  local copies, waits for them, and re-layouts  12.7 us (7%)
    pallas_call x1, Pallas kernels, run_layer(): pl.pallas_call(layer_kernel, out_shape=[jax.ShapeDtypeStruct(*shape) for...  168 us
    unnamed x27, local copies, waits for them, and re-layouts  11.4 us

profile of v3, /device:TPU:0, one launch (start us, length us, event | category | flops | bytes accessed | tf_op | source)
XLA Modules:
  0.0 181.7 jit_solution(13867559720928935727)
XLA Ops:
  0.7 0.0 copy-start.1
  0.7 2.0 %copy.38.refs_0_ = bf16[2,197,768]{2,1,0:T(8,128)(2,1)} copy(bf16[2,197,768]{2,0,1:T(2,128)(2,1)} %param.20) | data formatting | bytes 1210368 | tf_op args[0]
  2.7 0.0 copy-done.1
  2.7 0.9 copy.39.refs_3_
  3.6 168.3 %shard_map.331 = (bf16[2,197,768]{2,1,0:T(8,128)(2,1)}, bf16[2,197,768]{2,1,0:T(8,128)(2,1)}, f32[24,2304]{1,0:T(8,128)}, f32[24,768]{1,0:T(8,128)}, f32[96,768]...) custom-call(bf16[2,197,768]{2,1,0:T(8,128)(2,1)} %copy.38.refs_0_, ...), custom_call_target="tpu_custom_call" | custom-call | tf_op jit(solution)/shard_map/pallas_call | solution.py:833
  171.9 0.0 copy-start.7
  171.9 0.0 copy-start
  171.9 2.4 %copy.40 = bf16[2,197,768]{2,0,1:T(2,128)(2,1)} copy(bf16[2,197,768]{2,1,0:T(8,128)(2,1)} %get-tuple-element.36) | data formatting | bytes 1210368
  174.3 0.0 copy-done.7
  174.3 0.0 copy-start.8
  174.3 0.7 copy-done.8
  175.1 0.7 slice_reduce_fusion
  175.7 0.6 reshape.43
  176.3 0.0 copy-done
  176.3 0.0 copy-start.4
  176.3 1.3 copy.41
  177.6 0.0 copy-done.4
  177.6 0.0 copy-start.5
  177.6 0.0 copy-start.3
  177.6 0.7 copy.47
  178.3 0.2 copy-done.5
  178.5 0.6 copy.48
  179.2 0.0 copy-done.3
  179.2 0.0 copy-start.2
  179.2 0.7 copy.49
  179.9 0.4 copy-done.2
  180.3 0.0 copy-start.6
  180.3 0.7 copy.50
  181.0 0.1 copy-done.6
  181.0 0.6 copy.51
  (1 shorter events, 0.0 us)
Async XLA Ops:
  0.7 2.0 %copy-start.1 = (bf16[2,197,768]{2,0,1:T(2,128)(2,1)S(1)}, bf16[2,197,768]{2,0,1:T(2,128)(2,1)}, u32[]{:S(2)}) copy-start(bf16[2,197,768]{2,0,1:T(2,128)(2,1)} %param.23) | copy-start | bytes 1815556
  171.9 2.4 %copy-start.7 = (f32[16,768]{1,0:T(8,128)S(1)}, f32[16,768]{1,0:T(8,128)}, u32[]{:S(2)}) copy-start(f32[16,768]{1,0:T(8,128)} %get-tuple-element.34) | copy-start | bytes 147460
  171.9 4.5 %copy-start = (bf16[2,197,768]{2,1,0:T(8,128)(2,1)S(1)}, bf16[2,197,768]{2,1,0:T(8,128)(2,1)}, u32[]{:S(2)}) copy-start(bf16[2,197,768]{2,1,0:T(8,128)(2,1)} %get-tuple-element.37) | copy-start | bytes 1815556
  174.3 0.7 copy-start.8
  176.3 1.3 copy-start.4
  177.6 0.9 copy-start.5
  177.6 1.5 copy-start.3
  179.2 1.1 copy-start.2
  180.3 0.8 copy-start.6
